TPU v7x, 32 devices: a whole 2x2x4 slice. The times are simulated.
32 devices in a mesh: grp: 2 (over x), det: 16 (over z, y, core).
Axes of the slice: x: 2, y: 2, z: 4, core: 2. Of those that a mesh axis runs over, the one named last changes fastest.
Arguments:
- timestream: float32 [2, 1024, 16384], P('grp', 'det'), parts along dimension 0, may hold values from -6 to 6
- gains: float32 [2, 1024], P('grp', 'det'), parts along dimension 0, may hold values from 0.5 to 2
- mode_pattern: float32 [2048, 256], P('grp'), parts along dimension 0, may hold values from -0.375 to 0.375
- mode_weights: float32 [2048, 256], P('grp'), parts along dimension 0, may hold values from -0.1875 to 0.1875
- noise_weight: float32 [2048, 16384], P(('grp', 'det')), parts along dimension 0, may hold values from 0.05 to 1
- block_ids: int32 [2, 1024, 64], P('grp', 'det'), parts along dimension 0, may hold values from 0 to 255
- hits: int32 [2, 1024, 64], P('grp', 'det'), parts along dimension 0, may hold values from 0 to 3
- sky_rows: int32 [512], P('grp'), parts along dimension 0, may hold values from 0 to 255, each once
Outputs:
- filtered: float32 [2, 1024, 16384], P('grp', 'det'), parts along dimension 0
- sky_map: float32 [512, 256], P(('grp', 'det')), parts along dimension 0
There are 2 independent parts, one for each index of `grp`. A program takes and returns all parts, laid end to end along the dimension named above; each array names one. Nothing has to cross between parts.
Inputs may be any that keep to these rules, and one draw needn't show every extreme that they name: `sky_rows`: each row number appears exactly once.
All inputs are finite; a program needn't handle non-finite values.
Results may differ from a plain program's by a relative error of at most 0.000078.
Values sent between devices are 32-bit elements; how exact they have to be, the bound alone decides.
A program may use at most 128 MiB of HBM per device.

v0:
```python
import math

import jax
import jax.numpy as jnp
from jax import lax
from jax.sharding import PartitionSpec as P

SIDE = 128
PIX = 256


def dft_tables(side):
    first = lax.broadcasted_iota(jnp.int32, (side, side), 0)
    second = lax.broadcasted_iota(jnp.int32, (side, side), 1)
    angle = (first * second % side).astype(jnp.float32) * (2.0 * math.pi / side)
    return (jnp.cos(angle), jnp.sin(angle))


def twiddle_tables(side):
    first = lax.broadcasted_iota(jnp.int32, (side, side), 0)
    second = lax.broadcasted_iota(jnp.int32, (side, side), 1)
    angle = (first * second).astype(jnp.float32) * (2.0 * math.pi / (side * side))
    return (jnp.cos(angle), jnp.sin(angle))


def shards(timestream, gains, mode_pattern, mode_weights, noise_weight, block_ids, hits, sky_rows):
    highest = lax.Precision.HIGHEST
    det_local = timestream.shape[1]
    samples = timestream.shape[2]
    calibrated = timestream / gains[:, :, None]
    slab = lax.all_to_all(calibrated, "det", split_axis=2, concat_axis=1, tiled=True)
    coeff = jnp.einsum("dr,odc->orc", mode_weights, slab, precision=highest)
    corrected = slab - jnp.einsum("dr,orc->odc", mode_pattern, coeff, precision=highest)
    cos_table, sin_table = dft_tables(SIDE)
    twist_cos, twist_sin = twiddle_tables(SIDE)
    spectral_weight = noise_weight.reshape(det_local, SIDE, SIDE)
    slab = lax.all_to_all(corrected, "det", split_axis=1, concat_axis=2, tiled=True)
    items = slab.shape[0]
    signal = slab.reshape(items * det_local, SIDE, SIDE)
    section_real = jnp.einsum("kn,rnm->rkm", cos_table, signal, precision=highest)
    section_imag = -jnp.einsum("kn,rnm->rkm", sin_table, signal, precision=highest)
    turned_real = section_real * twist_cos + section_imag * twist_sin
    turned_imag = section_imag * twist_cos - section_real * twist_sin
    freq_real = jnp.einsum("rkn,nj->rjk", turned_real, cos_table, precision=highest) + jnp.einsum(
        "rkn,nj->rjk", turned_imag, sin_table, precision=highest
    )
    freq_imag = jnp.einsum("rkn,nj->rjk", turned_imag, cos_table, precision=highest) - jnp.einsum(
        "rkn,nj->rjk", turned_real, sin_table, precision=highest
    )
    freq_real = (freq_real.reshape(items, det_local, SIDE, SIDE) * spectral_weight).reshape(
        items * det_local, SIDE, SIDE
    )
    freq_imag = (freq_imag.reshape(items, det_local, SIDE, SIDE) * spectral_weight).reshape(
        items * det_local, SIDE, SIDE
    )
    back_real = jnp.einsum("rjk,jm->rkm", freq_real, cos_table, precision=highest) - jnp.einsum(
        "rjk,jm->rkm", freq_imag, sin_table, precision=highest
    )
    back_imag = jnp.einsum("rjk,jm->rkm", freq_imag, cos_table, precision=highest) + jnp.einsum(
        "rjk,jm->rkm", freq_real, sin_table, precision=highest
    )
    final_real = back_real * twist_cos - back_imag * twist_sin
    final_imag = back_imag * twist_cos + back_real * twist_sin
    result = jnp.einsum("nk,rkm->rnm", cos_table, final_real, precision=highest) - jnp.einsum(
        "nk,rkm->rnm", sin_table, final_imag, precision=highest
    )
    filtered = (result / samples).reshape(items, det_local, samples)
    tile_rows = filtered.reshape(-1, PIX)
    weight = hits.reshape(-1).astype(jnp.float32)
    ids_flat = block_ids.reshape(-1)
    blocks = sky_rows.shape[0]
    ladder = lax.broadcasted_iota(jnp.int32, (blocks, ids_flat.shape[0]), 0)
    rows = jnp.sum(jnp.where(ids_flat[None, :] == ladder, sky_rows[:, None], 0), axis=0)
    table = jnp.where(rows[None, :] == ladder, weight[None, :], 0.0)
    sums = jnp.dot(table, tile_rows, precision=highest, preferred_element_type=jnp.float32)
    counts = jnp.sum(table, axis=1)
    own_sums, own_counts = (
        lax.psum_scatter(sums, "det", scatter_dimension=0, tiled=True),
        lax.psum_scatter(counts, "det", scatter_dimension=0, tiled=True),
    )
    sky_map = own_sums / jnp.sqrt(1.0 + own_counts)[:, None]
    return (filtered, sky_map)


def solution(mesh):
    in_specs = (
        P("grp", "det", None),
        P("grp", "det"),
        P("grp", None),
        P("grp", None),
        P(("grp", "det"), None),
        P("grp", "det", None),
        P("grp", "det", None),
        P("grp"),
    )
    out_specs = (P("grp", "det", None), P(("grp", "det"), None))
    return jax.shard_map(shards, mesh=mesh, in_specs=in_specs, out_specs=out_specs, check_vma=False)
```

profile of v0, /device:TPU:0, one launch (start us, length us, event | category | flops | bytes accessed | tf_op | source)
XLA Modules:
  0.0 557.3 jit_solution(1143022647342395061)
XLA Ops:
  11.9 17.1 %copy.141 = f32[1,64,16384]{1,0,2:T(1,128)} copy(f32[1,64,16384]{2,1,0:T(8,128)} %broadcast_divide_fusion) | data formatting | bytes 8388608 | tf_op jit(solution)/shard_map/div | solution.py:30
  29.5 74.5 %reduce = f32[16384,64]{1,0:T(8,128)} reduce(f32[16384,1,64]{2,1,0:T(1,128)} %bitcast.98, f32[]{:T(128)} %broadcast.67), dimensions={1}, to_apply=%bitcast.83.reduce_sub_computation | reduce | bytes 8388612
  103.9 13.3 %reshape.70 = f32[16,1,65536]{2,1,0:T(1,128)} reshape(f32[16384,64]{1,0:T(8,128)} %reduce) | data formatting | bytes 8388608
  117.2 100.1 %all_to_all.33 = f32[16,1,65536]{2,1,0:T(1,128)} all-to-all(f32[16,1,65536]{2,1,0:T(1,128)} %reshape.70), channel_id=1, replica_groups=mesh['grp'=2,'det'=16] {'det'}, dimensions={0} | all-to-all | bytes 8388608 | tf_op jit(solution)/shard_map/all_to_all | solution.py:31
  217.3 13.8 %reduce.1 = f32[16,65536]{1,0:T(8,128)} reduce(f32[16,1,65536]{2,1,0:T(1,128)} %all_to_all.33, f32[]{:T(128)} %broadcast.67), dimensions={1}, to_apply=%all_to_all.24.reduce_sub_computation | reduce | bytes 8388612 | tf_op jit(solution)/shard_map/all_to_all | solution.py:31
  231.1 14.0 %reshape.71 = f32[16384,1,64]{2,1,0:T(1,128)} reshape(f32[16,65536]{1,0:T(8,128)} %reduce.1) | data formatting | bytes 8388608
  245.1 7.3 %copy.189 = f32[1,64,16,1024]{3,2,1,0:T(8,128)} copy(f32[1,64,16,1024]{1,3,2,0:T(8,128)} %bitcast.99) | data formatting | bytes 8388608 | tf_op jit(solution)/shard_map/all_to_all | solution.py:31
  252.4 6.5 %copy.143 = f32[1,16,64,1024]{3,2,1,0:T(8,128)} copy(f32[1,16,64,1024]{3,1,2,0:T(8,128)} %bitcast.100) | data formatting | bytes 8388608 | tf_op jit(solution)/shard_map/all_to_all | solution.py:31
  258.9 5.4 copy.145
  264.4 19.2 %convolution_bitcast_fusion = f32[256,1024]{0,1:T(8,128)S(1)} fusion(f32[1024,1024]{1,0:T(8,128)} %bitcast.97, f32[1024,256]{1,0:T(8,128)S(1)} %copy-done.5), kind=kOutput, calls=%fused_computation.34 | convolution fusion | flops 3221225472 | bytes 6291456 | tf_op jit(solution)/shard_map/dr,odc->orc/dot_general | solution.py:32
  283.6 5.2 bitcast_subtract_fusion
  288.8 11.0 %copy.146 = f32[1,1024,1024]{2,0,1:T(1,128)} copy(f32[1,1024,1024]{1,2,0:T(8,128)} %bitcast_subtract_fusion) | data formatting | bytes 8388608 | tf_op jit(solution)/shard_map/sub | solution.py:33
  299.8 5.3 all-to-all-start.1
  311.8 71.0 %all-to-all-done.1 = f32[1,1024,1024]{2,0,1:T(1,128)} async-done(((f32[1,1024,1024]{2,0,1:T(1,128)}), f32[1,1024,1024]{2,0,1:T(1,128)}, u32[]{:S(2)}, u32[]{:S(2)}) %all-to-all-start.1) | async-done | bytes 4194336 | tf_op jit(solution)/shard_map/all_to_all | solution.py:37
  395.3 9.5 %fusion.35 = f32[64,128,128]{2,1,0:T(8,128)S(1)} fusion(f32[64,128,128]{2,1,0:T(8,128)} %reshape.61), kind=kOutput, calls=%fused_computation.48 | convolution fusion | flops 1610842112 | bytes 8388608 | tf_op jit(solution)/shard_map/kn,rnm->rkm/dot_general | solution.py:41
  404.8 7.0 %fusion.43 = f32[64,128,128]{2,1,0:T(8,128)S(1)} fusion(f32[64,128,128]{2,1,0:T(8,128)S(1)} %copy-done.3), kind=kOutput, calls=%fused_computation.56 | convolution fusion | flops 1610842112 | bytes 8388608 | tf_op jit(solution)/shard_map/kn,rnm->rkm/dot_general | solution.py:40
  431.2 5.2 bitcast_multiply_fusion.1
  441.0 5.1 convolution_add_fusion
  454.9 5.7 %multiply_bitcast_fusion = f32[64,128,128]{1,2,0:T(8,128)} fusion(f32[64,128,128]{2,1,0:T(8,128)S(1)} %fusion.4, f32[64,128,128]{1,2,0:T(8,128)S(1)} %convolution_add_fusion, f32[64,128,128]{1,2,0:T(8,128)S(1)} %convolution_subtract_fusion, f32[128,128]{0,1:T(8,128)S(1)} %copy.151, f32[128,128]{0,1:T(8,128)S(1)} %copy.149), kind=kOutput, calls=%fused_computation.15 | convolution fusion | flops 1616084992 | bytes 16908288 | tf_op jit(solution)/shard_map/nk,rkm->rnm/dot_general | solution.py:64
  460.7 5.8 %copy.168 = f32[64,128,128]{2,1,0:T(8,128)} copy(f32[64,128,128]{1,2,0:T(8,128)} %multiply_bitcast_fusion) | data formatting | bytes 8388608 | tf_op jit(solution)/shard_map/div | solution.py:67
  466.4 5.2 reshape_reshape.3
  471.6 6.9 %fusion = f32[256,256]{1,0:T(8,128)} fusion(f32[4096,256]{1,0:T(8,128)} %reshape_reshape.3, f32[4096]{0:T(1024)S(1)} %convert_element_type.62, s32[4096]{0:T(1024)S(1)} %select_reduce_fusion.1), kind=kOutput, calls=%fused_computation.1 | convolution fusion | flops 3223322624 | bytes 4489216 | tf_op jit(solution)/shard_map/dot_general | solution.py:75
  480.4 47.6 %all-reduce = f32[256]{0:T(256)S(1)} all-reduce(f32[256]{0:T(256)S(1)} %select_reduce_fusion), channel_id=3, replica_groups=mesh['grp'=2,'det'=16] {'det'}, use_global_device_ids=true, to_apply=%region_3.4.clone | all-reduce | flops 256 | bytes 2048
  533.1 15.8 %reduce-scatter.2.cloned.1.call-done = f32[16,256]{1,0:T(8,128)} async-done(((f32[256,256]{1,0:T(8,128)}), f32[16,256]{1,0:T(8,128)}) %reduce-scatter.2.cloned.1.call-update) | async-done | bytes 16400 | tf_op jit(solution)/shard_map/reduce_scatter | solution.py:78
  (48 shorter events, 64.6 us)
Async XLA Ops:
  7.2 276.4 %copy-start = (f32[1024,256]{1,0:T(8,128)S(1)}, f32[1024,256]{1,0:T(8,128)}, u32[]{:S(2)}) copy-start(f32[1024,256]{1,0:T(8,128)} %param.10) | copy-start | bytes 3145732
  258.9 5.4 copy-start.5
  264.4 19.2 %copy-start.4 = (f32[1,1024,1024]{1,2,0:T(8,128)S(1)}, f32[1,1024,1024]{1,2,0:T(8,128)}, u32[]{:S(2)}) copy-start(f32[1,1024,1024]{1,2,0:T(8,128)} %copy.145) | copy-start | bytes 12582916
  299.8 83.0 %all-to-all-start.1 = ((f32[1,1024,1024]{2,0,1:T(1,128)}), f32[1,1024,1024]{2,0,1:T(1,128)}, u32[]{:S(2)}, u32[]{:S(2)}) async-start(f32[1,1024,1024]{2,0,1:T(1,128)} %copy.146), calls=%async_computation.1 | async-start | bytes 8388608 | tf_op jit(solution)/shard_map/all_to_all | solution.py:37
  305.1 243.8 %reduce-scatter.2.cloned.1.call-start = ((), (), s32[]{:S(2)}) async-start(), calls=%async_computation.3 | async-start | bytes 278528 | tf_op jit(solution)/shard_map/reduce_scatter | solution.py:78
  305.8 5.0 copy-start.7
  305.9 5.1 copy-start.6
  305.9 5.1 copy-start.8
  395.3 9.5 %copy-start.3 = (f32[64,128,128]{2,1,0:T(8,128)S(1)}, f32[64,128,128]{2,1,0:T(8,128)}, u32[]{:S(2)}) copy-start(f32[64,128,128]{2,1,0:T(8,128)} %reshape.61) | copy-start | bytes 12582916
  416.5 4.8 copy-start.2
  471.6 6.9 %copy-start.9 = (u32[32]{0:T(128)S(1)}, u32[32]{0:T(128)}, u32[]{:S(2)}) copy-start(u32[32]{0:T(128)} %constant.33) | copy-start | bytes 388
  528.0 22.3 %copy-start.1 = (f32[1024,256]{1,0:T(8,128)S(1)}, f32[1024,256]{1,0:T(8,128)}, u32[]{:S(2)}) copy-start(f32[1024,256]{1,0:T(8,128)} %param.10) | copy-start | bytes 3145732
Sparse Core Ops, SparseCore 0:
  478.6 70.2 reduce-scatter.1
where the time goes:
time: 558 us; the launch traced here: 557 us
  blocking collectives  148 us (27%)
  local copies, waits for them, and re-layouts  109 us (20%)
  matrix products  96.5 us (17%)
  other arithmetic  96.2 us (17%)
  waiting for transfers between devices  86.8 us (16%)
  between operations  15.1 us (3%)
    all_to_all x1, blocking collectives, shards(): lax.all_to_all(calibrated, 'det', split_axis=2, concat_axis=1, tiled=True)  100 us
    unnamed x1, other arithmetic  74.5 us
    all_to_all x1, waiting for transfers between devices, shards(): lax.all_to_all(corrected, 'det', split_axis=1, concat_axis=2, tiled=True)  71 us
    unnamed x1, blocking collectives  47.6 us
    unnamed x26, local copies, waits for them, and re-layouts  36.5 us
    all_to_all x3, local copies, waits for them, and re-layouts, shards(): lax.all_to_all(calibrated, 'det', split_axis=2, concat_axis=1, tiled=True)  19.3 us
    dot_general x1, matrix products, shards(): coeff = jnp.einsum('dr,odc->orc', mode_weights, slab, precision=highest)  19.2 us
    div x1, local copies, waits for them, and re-layouts, shards(): calibrated = timestream / gains[:, :, None]  17.1 us
  transfers between devices with their start and end apart: 2, of which 2 were waited for; matrix products, arithmetic and copies ran while one was open for 2% of the time, Pallas kernels for 0%

commit v1 on v0

v1 whole, which is shorter than its diff:
```python
import functools
import math

import jax
import jax.numpy as jnp
import ml_dtypes
import numpy as np
from jax import lax
from jax.experimental import pallas as pl
from jax.experimental.pallas import tpu as pltpu
from jax.sharding import PartitionSpec as P

PIX = 256
LANES = 128
MIB = 1 << 20


def split(value):
    high = value.astype(jnp.bfloat16)
    return high, (value - high.astype(jnp.float32)).astype(jnp.bfloat16)


def product(left, right):
    dot = functools.partial(jnp.dot, preferred_element_type=jnp.float32)
    return dot(left[0], right[0]) + (dot(left[0], right[1]) + dot(left[1], right[0]))


def halves(table):
    high = table.astype(ml_dtypes.bfloat16)
    low = (table - high.astype(np.float64)).astype(ml_dtypes.bfloat16)
    return np.stack([high, low])


def transform_tables(side):
    index = np.arange(side)
    angle = (np.outer(index, index) % side) * (2.0 * math.pi / side)
    cos, sin = np.cos(angle), np.sin(angle)
    twist = np.outer(index, index) * (2.0 * math.pi / (side * side))
    turn = np.stack([np.cos(twist), np.sin(twist)]).astype(np.float32)
    last = np.concatenate([cos, -sin], 1) / (side * side)
    per_row = PIX // side
    last = last.reshape(side // per_row, per_row, 2 * side).swapaxes(0, 1).reshape(side, 2 * side)
    return (
        halves(np.concatenate([cos, -sin], 0)),
        halves(np.block([[cos, -sin], [sin, cos]])),
        halves(np.block([[cos, sin], [-sin, cos]])),
        halves(last),
        turn,
    )


def correct_kernel(
    plane, planes, chunks, x_ref, gain_ref, weight_ref, pattern_ref, out_ref,
    cal, slab, part, to_right, to_left, from_left, from_right, back,
    raw_send, raw_recv, right_send, right_recv, left_send, left_recv, back_send, back_recv,
):
    me = lax.axis_index("det")
    z, q = me // plane, me % plane
    dets, samples = x_ref.shape
    quarter = samples // plane
    width = quarter // chunks
    first, last = z == 0, z == planes - 1

    barrier = pltpu.get_barrier_semaphore()

    def partner(step):
        return lax.rem(q + step, plane)

    for step in range(1, plane):
        pl.semaphore_signal(barrier, inc=1, device_id={"det": z * plane + partner(step)})

    @pl.when(z > 0)
    def _():
        pl.semaphore_signal(barrier, inc=1, device_id={"det": me - plane})

    @pl.when(z < planes - 1)
    def _():
        pl.semaphore_signal(barrier, inc=1, device_id={"det": me + plane})

    at_ends = (z == 0).astype(jnp.int32) + (z == planes - 1).astype(jnp.int32)
    pl.semaphore_wait(barrier, plane + 1 - at_ends)

    def span(owner, chunk):
        return pl.ds(pl.multiple_of(owner * quarter + chunk * width, width), width)

    def raw_copy(chunk, step):
        other = partner(step)
        return pltpu.make_async_remote_copy(
            src_ref=cal.at[:, span(other, chunk)],
            dst_ref=slab.at[chunk, pl.ds(pl.multiple_of(q * dets, 8), dets), :],
            send_sem=raw_send.at[chunk, step - 1],
            recv_sem=raw_recv.at[chunk, step - 1],
            device_id={"det": z * plane + other},
        )

    def back_copy(chunk, step):
        other = partner(step)
        return pltpu.make_async_remote_copy(
            src_ref=back.at[chunk, pl.ds(pl.multiple_of(other * dets, 8), dets), :],
            dst_ref=out_ref.at[:, span(q, chunk)],
            send_sem=back_send.at[chunk, step - 1],
            recv_sem=back_recv.at[chunk, step - 1],
            device_id={"det": z * plane + other},
        )

    def right_copy(chunk):
        return pltpu.make_async_remote_copy(
            src_ref=to_right.at[chunk],
            dst_ref=from_left.at[chunk],
            send_sem=right_send.at[chunk],
            recv_sem=right_recv.at[chunk],
            device_id={"det": lax.rem(me + plane, plane * planes)},
        )

    def left_copy(chunk):
        return pltpu.make_async_remote_copy(
            src_ref=to_left.at[chunk],
            dst_ref=from_right.at[chunk],
            send_sem=left_send.at[chunk],
            recv_sem=left_recv.at[chunk],
            device_id={"det": lax.rem(me + plane * (planes - 1), plane * planes)},
        )

    own_rows = pl.ds(pl.multiple_of(q * dets, 8), dets)

    def send_raw(chunk, carry):
        for owner in range(plane):
            cal[:, span(owner, chunk)] = x_ref[:, span(owner, chunk)] / gain_ref[...]
        for step in range(1, plane):
            raw_copy(chunk, step).start()
        slab[chunk, own_rows, :] = cal[:, span(q, chunk)]
        return carry

    lax.fori_loop(0, chunks, send_raw, 0)

    weight = split(weight_ref[...])
    pattern = split(pattern_ref[...])

    def one_step(i, carry):
        @pl.when(i < chunks)
        def _():
            for step in range(1, plane):
                raw_copy(i, step).wait_recv()
            part[i] = product(weight, split(slab[i]))

        c_right = i - z

        @pl.when((c_right >= 0) & (c_right < chunks))
        def _():
            @pl.when(first)
            def _():
                from_left[c_right] = jnp.zeros(part.shape[1:], jnp.float32)
                to_right[c_right] = part[c_right]

            @pl.when(z > 0)
            def _():
                right_copy(c_right).wait_recv()
                to_right[c_right] = part[c_right] + from_left[c_right]

            @pl.when(z < planes - 1)
            def _():
                right_copy(c_right).start()

        c_left = i - (planes - 1 - z)

        @pl.when((c_left >= 0) & (c_left < chunks))
        def _():
            @pl.when(last)
            def _():
                from_right[c_left] = jnp.zeros(part.shape[1:], jnp.float32)
                to_left[c_left] = part[c_left]

            @pl.when(z < planes - 1)
            def _():
                left_copy(c_left).wait_recv()
                to_left[c_left] = part[c_left] + from_right[c_left]

            @pl.when(z > 0)
            def _():
                left_copy(c_left).start()

        c = i - (planes - 1)

        @pl.when(c >= 0)
        def _():
            coeff = to_right[c] + from_right[c]
            back[c] = slab[c] - product(pattern, split(coeff))
            for step in range(1, plane):
                back_copy(c, step).start()
            out_ref[:, span(q, c)] = back[c, own_rows, :]

        return carry

    lax.fori_loop(0, chunks + planes - 1, one_step, 0)

    def finish(chunk, carry):
        for step in range(1, plane):
            back_copy(chunk, step).wait_recv()
            back_copy(chunk, step).wait_send()
            raw_copy(chunk, step).wait_send()

        @pl.when(z < planes - 1)
        def _():
            right_copy(chunk).wait_send()

        @pl.when(z > 0)
        def _():
            left_copy(chunk).wait_send()

        return carry

    lax.fori_loop(0, chunks, finish, 0)


def correct(stream, gains, mode_pattern, mode_weights, size):
    dets, samples = stream.shape
    rank = mode_pattern.shape[1]
    plane = 4 if size % 4 == 0 else 1
    planes = size // plane
    quarter = samples // plane
    chunks = max(1, quarter // 256)
    width = quarter // chunks
    rows = plane * dets
    start = (lax.axis_index("det") // plane) * rows
    weights = lax.dynamic_slice_in_dim(mode_weights, start, rows, 0).T
    pattern = lax.dynamic_slice_in_dim(mode_pattern, start, rows, 0)
    f32 = jnp.float32
    sem = pltpu.SemaphoreType.DMA
    coeffs = pltpu.VMEM((chunks, rank, width), f32)
    block = pltpu.VMEM((chunks, rows, width), f32)
    return pl.pallas_call(
        functools.partial(correct_kernel, plane, planes, chunks),
        out_shape=jax.ShapeDtypeStruct((dets, samples), f32),
        in_specs=[pl.BlockSpec(memory_space=pltpu.VMEM)] * 4,
        out_specs=pl.BlockSpec(memory_space=pltpu.VMEM),
        scratch_shapes=[
            pltpu.VMEM((dets, samples), f32), block, coeffs, coeffs, coeffs, coeffs, coeffs, block,
            sem((chunks, plane)), sem((chunks, plane)), sem((chunks,)), sem((chunks,)),
            sem((chunks,)), sem((chunks,)), sem((chunks, plane)), sem((chunks, plane)),
        ],
        compiler_params=pltpu.CompilerParams(
            collective_id=0, has_side_effects=True, vmem_limit_bytes=56 * MIB
        ),
        name="correct",
    )(stream, gains.reshape(dets, 1), weights, pattern)


def filter_kernel(x_ref, w_ref, row_ref, hit_ref, t1, t2, t3, t4, turn, out_ref, acc_ref):
    batch, side, _ = x_ref.shape
    per_row = PIX // side
    tiles = side // per_row
    cos, sin = turn[0], turn[1]
    signal = jnp.concatenate([x_ref[b] for b in range(batch)], axis=1)
    section = product((t1[0], t1[1]), split(signal))
    turned = []
    for b in range(batch):
        real, imag = section[:side, b * side:(b + 1) * side], section[side:, b * side:(b + 1) * side]
        turned.append(jnp.concatenate([real * cos + imag * sin, imag * cos - real * sin], axis=1))
    freq = product(split(jnp.concatenate(turned, axis=0)), (t2[0], t2[1]))
    weighted = []
    for b in range(batch):
        weight = w_ref[b].T
        weighted.append(freq[b * side:(b + 1) * side] * jnp.concatenate([weight, weight], axis=1))
    section = product(split(jnp.concatenate(weighted, axis=0)), (t3[0], t3[1]))
    turned = []
    for b in range(batch):
        real, imag = section[b * side:(b + 1) * side, :side], section[b * side:(b + 1) * side, side:]
        turned.append(jnp.concatenate([real * cos - imag * sin, imag * cos + real * sin], axis=0))
    result = product((t4[0], t4[1]), split(jnp.concatenate(turned, axis=1)))
    tiled = []
    for b in range(batch):
        column = result[:, b * side:(b + 1) * side]
        tiled.append(jnp.concatenate([column[p * tiles:(p + 1) * tiles] for p in range(per_row)], axis=1))
        out_ref[b] = tiled[b]
    high, low = split(jnp.concatenate(tiled, axis=0))
    blocks = acc_ref.shape[0]
    ladder = lax.broadcasted_iota(jnp.int32, (blocks, batch * tiles), 0)
    table = jnp.where(row_ref[...] == ladder, hit_ref[...], 0.0)
    half = table.astype(jnp.bfloat16)
    dot = functools.partial(jnp.dot, preferred_element_type=jnp.float32)
    sums = dot(half, high) + dot(half, low)
    counts = table[:, :LANES]
    for at in range(LANES, batch * tiles, LANES):
        counts = counts + table[:, at:at + LANES]

    @pl.when(pl.program_id(0) == 0)
    def _():
        acc_ref[...] = jnp.zeros_like(acc_ref)

    acc_ref[:, :PIX] += sums
    acc_ref[:, PIX:] += counts


def filter_and_bin(signal, weight, rows, hits, blocks):
    dets, side, _ = signal.shape
    tables = transform_tables(side)
    batch = 4
    tiles = side * side // PIX
    whole = lambda table: pl.BlockSpec(table.shape, lambda i: (0,) * table.ndim)
    cube = pl.BlockSpec((batch, side, side), lambda i: (i, 0, 0))
    line = pl.BlockSpec((1, batch * tiles), lambda i: (0, i))
    return pl.pallas_call(
        filter_kernel,
        grid=(dets // batch,),
        out_shape=(
            jax.ShapeDtypeStruct((dets, tiles, PIX), jnp.float32),
            jax.ShapeDtypeStruct((blocks, PIX + LANES), jnp.float32),
        ),
        in_specs=[cube, cube, line, line] + [whole(table) for table in tables],
        out_specs=(
            pl.BlockSpec((batch, tiles, PIX), lambda i: (i, 0, 0)),
            pl.BlockSpec((blocks, PIX + LANES), lambda i: (0, 0)),
        ),
        compiler_params=pltpu.CompilerParams(vmem_limit_bytes=48 * MIB),
        name="filter_bin",
    )(signal, weight, rows, hits, *[jnp.asarray(table) for table in tables])


def map_kernel(size, acc_ref, out_ref, landed, send_sem, recv_sem):
    me = lax.axis_index("det")
    rows = out_ref.shape[0]
    barrier = pltpu.get_barrier_semaphore()

    def greet(step, carry):
        pl.semaphore_signal(barrier, inc=1, device_id={"det": lax.rem(me + step, size)})
        return carry

    lax.fori_loop(1, size, greet, 0)
    pl.semaphore_wait(barrier, size - 1)

    def copy(step):
        other = lax.rem(me + step, size)
        return pltpu.make_async_remote_copy(
            src_ref=acc_ref.at[pl.ds(pl.multiple_of(other * rows, 8), rows), :],
            dst_ref=landed.at[step],
            send_sem=send_sem.at[step],
            recv_sem=recv_sem.at[step],
            device_id={"det": other},
        )

    def start(step, carry):
        copy(step).start()
        return carry

    lax.fori_loop(1, size, start, 0)

    def add(step, total):
        copy(step).wait_recv()
        return total + landed[step]

    own = acc_ref[pl.ds(pl.multiple_of(me * rows, 8), rows), :]
    total = lax.fori_loop(1, size, add, own)
    counts = jnp.sum(total[:, PIX:], axis=1, keepdims=True)
    out_ref[...] = total[:, :PIX] / jnp.sqrt(1.0 + counts)

    def finish(step, carry):
        copy(step).wait_send()
        return carry

    lax.fori_loop(1, size, finish, 0)


def combine_map(acc, size):
    blocks, columns = acc.shape
    rows = blocks // size
    return pl.pallas_call(
        functools.partial(map_kernel, size),
        out_shape=jax.ShapeDtypeStruct((rows, PIX), jnp.float32),
        in_specs=[pl.BlockSpec(memory_space=pltpu.VMEM)],
        out_specs=pl.BlockSpec(memory_space=pltpu.VMEM),
        scratch_shapes=[
            pltpu.VMEM((size, rows, columns), jnp.float32),
            pltpu.SemaphoreType.DMA((size,)),
            pltpu.SemaphoreType.DMA((size,)),
        ],
        compiler_params=pltpu.CompilerParams(collective_id=1, has_side_effects=True),
        name="combine_map",
    )(acc)


def shards(size, timestream, gains, mode_pattern, mode_weights, noise_weight, block_ids, hits, sky_rows):
    items, dets, samples = timestream.shape
    side = math.isqrt(samples)
    ids_flat = block_ids.reshape(-1)
    blocks = sky_rows.shape[0]
    ladder = lax.broadcasted_iota(jnp.int32, (blocks, ids_flat.shape[0]), 0)
    rows = jnp.sum(jnp.where(ids_flat[None, :] == ladder, sky_rows[:, None], 0), axis=0)
    weight = hits.reshape(1, -1).astype(jnp.float32)
    corrected = correct(timestream.reshape(items * dets, samples), gains.reshape(-1), mode_pattern, mode_weights, size)
    filtered, acc = filter_and_bin(
        corrected.reshape(dets, side, side), noise_weight.reshape(dets, side, side), rows[None, :], weight, blocks
    )
    return (filtered.reshape(items, dets, samples), combine_map(acc, size))


def solution(mesh):
    in_specs = (
        P("grp", "det", None),
        P("grp", "det"),
        P("grp", None),
        P("grp", None),
        P(("grp", "det"), None),
        P("grp", "det", None),
        P("grp", "det", None),
        P("grp"),
    )
    out_specs = (P("grp", "det", None), P(("grp", "det"), None))
    body = functools.partial(shards, mesh.shape["det"])
    return jax.shard_map(body, mesh=mesh, in_specs=in_specs, out_specs=out_specs, check_vma=False)
```

time: 558 us -> 202 us (0.36)
  Pallas kernels: 0 us -> 173 us
  blocking collectives: 148 us -> 0 us
  matrix products: 96.5 us -> 0 us
  other arithmetic: 96.2 us -> 2.18 us
  local copies, waits for them, and re-layouts: 109 us -> 21.6 us
  waiting for transfers between devices: 86.8 us -> 0 us
  between operations: 15.1 us -> 0.74 us
    pallas_call x0 -> x3, Pallas kernels: none -> 173 us  [the longest x1 134 us: correct(): pl.pallas_call(functools.partial(correct_kernel, plane, planes, chunks),...]
    all_to_all x1 -> x0, blocking collectives: 100 us -> none  [shards(): lax.all_to_all(calibrated, 'det', split_axis=2, concat_axis=1, tiled=True)]
    dot_general x15 -> x0, matrix products: 96.5 us -> none  [the longest x1 19.2 us: shards(): coeff = jnp.einsum('dr,odc->orc', mode_weights, slab, precision=highest)]
    unnamed x1 -> x0, other arithmetic: 74.5 us -> none
    all_to_all x1 -> x0, waiting for transfers between devices: 71 us -> none  [shards(): lax.all_to_all(corrected, 'det', split_axis=1, concat_axis=2, tiled=True)]
    unnamed x1 -> x0, blocking collectives: 47.6 us -> none
    unnamed x26 -> x20, local copies, waits for them, and re-layouts: 36.5 us -> 12.6 us
    all_to_all x4 -> x0, local copies, waits for them, and re-layouts: 23.6 us -> none  [the longest x3 19.3 us: shards(): lax.all_to_all(calibrated, 'det', split_axis=2, concat_axis=1, tiled=True)]
  transfers between devices with their start and end apart: 2 -> 0, of which waited for: 2 -> 0; matrix products, arithmetic and copies ran while one was open for 2% -> 0% of each run, Pallas kernels for 0% -> 0%
where the time goes in v1:
time: 202 us; the launch traced here: 198 us
  Pallas kernels  173 us (86%)
  local copies, waits for them, and re-layouts  21.6 us (11%)
  other arithmetic  2.18 us (1%)
    pallas_call x1, Pallas kernels, correct(): pl.pallas_call(functools.partial(correct_kernel, plane, planes, chunks),...  134 us
    pallas_call x1, Pallas kernels, filter_and_bin(): pl.pallas_call(filter_kernel, grid=(dets // batch,), out_shape=(jax.Shape...  30.3 us
    unnamed x20, local copies, waits for them, and re-layouts  12.6 us
    pallas_call x1, Pallas kernels, combine_map(): pl.pallas_call(functools.partial(map_kernel, size), out_shape=jax.ShapeDt...  9.33 us
    reshape x1, local copies, waits for them, and re-layouts, shards(): return (filtered.reshape(items, dets, samples), combine_map(acc, size))  4.94 us

profile of v1, /device:TPU:0, one launch (start us, length us, event | category | flops | bytes accessed | tf_op | source)
XLA Modules:
  0.0 198.0 jit_solution(15441429364935144272)
XLA Ops:
  0.6 0.8 eq.10
  1.5 1.4 select_reduce_fusion
  2.9 1.3 copy.18.gain_ref
  4.3 0.8 convert_element_type.5
  5.0 0.1 convert_element_type.6.hit_ref
  5.1 1.8 constant_dynamic-slice_fusion
  6.9 0.8 copy.19
  7.7 133.8 %correct.1 = f32[64,16384]{1,0:T(8,128)} custom-call(f32[64,16384]{1,0:T(8,128)} %bitcast.12, f32[64,1]{1,0:T(8,128)} %copy.18.gain_ref, f32[256,256]{1,0:T(8,128)} %bitcast.14, f32[256,256]{1,0:T(8,128)} %get-tuple-element.6.pattern_ref), custom_call_target="tpu_custom_call" | custom-call | tf_op jit(solution)/shard_map/correct/pallas_call | solution.py:231
  141.5 0.0 copy-start.7
  141.6 5.1 %copy.20 = f32[8,8,128,128]{3,2,1,0:T(8,128)} copy(f32[8,8,128,128]{3,1,2,0:T(8,128)} %bitcast.11) | data formatting | bytes 8388608
  146.7 0.0 copy-done.7
  146.7 0.0 copy-start.5
  146.7 0.0 copy-start.6
  146.7 2.7 %copy.21 = f32[8,8,128,128]{3,2,1,0:T(8,128)} copy(f32[8,8,128,128]{3,1,2,0:T(8,128)S(1)} %bitcast.13) | data formatting | bytes 8388608
  149.4 0.0 copy-done.2
  149.4 0.0 copy-done.3
  149.4 0.0 copy-done.4
  149.4 0.0 copy-done.5
  149.4 30.3 %filter_bin.1 = (f32[64,64,256]{2,1,0:T(8,128)S(1)}, f32[256,384]{1,0:T(8,128)S(1)}) custom-call(f32[64,128,128]{2,1,0:T(8,128)} %bitcast.9, f32[64,128,128]{2,1,0:T(8,128)} %bitcast.10, s32[1,4096]{1,0:T(1,128)S(1)} %bitcast.8, f32[1,4096]{1,0:T(1,128)S(1)} %convert_element_type.6.hit_ref, bf16[2,256,128]{2,1,0:T(8,128)(2,1)S(1)} %copy-done.6, ...), custom_call_target="tpu_custom_call" | custom-call | tf_op jit(solution)/shard_map/filter_bin/pallas_call | solution.py:302
  179.7 1.9 copy-done
  181.7 0.7 copy-done.1
  182.4 4.9 %reshape.35 = f32[1,64,16384]{2,1,0:T(8,128)} reshape(f32[64,64,256]{2,1,0:T(8,128)} %copy-done) | data formatting | bytes 8388608 | tf_op jit(solution)/shard_map/reshape | solution.py:393
  187.3 9.3 %combine_map.1 = f32[16,256]{1,0:T(8,128)} custom-call(f32[256,384]{1,0:T(8,128)} %copy-done.1), custom_call_target="tpu_custom_call" | custom-call | tf_op jit(solution)/shard_map/combine_map/pallas_call | solution.py:366
  196.7 1.3 copy.23
  (6 shorter events, 0.0 us)
Async XLA Ops:
  141.5 5.1 %copy-start.7 = (f32[64,16384]{1,0:T(8,128)S(1)}, f32[64,16384]{1,0:T(8,128)}, u32[]{:S(2)}) copy-start(f32[64,16384]{1,0:T(8,128)} %param.17) | copy-start | bytes 12582916
  146.7 2.7 %copy-start.2 = (bf16[2,256,256]{2,1,0:T(8,128)(2,1)S(1)}, bf16[2,256,256]{2,1,0:T(8,128)(2,1)}, u32[]{:S(2)}) copy-start(bf16[2,256,256]{2,1,0:T(8,128)(2,1)} %constant.37.clone.t3) | copy-start | bytes 786436
  146.7 2.7 %copy-start.3 = (bf16[2,256,256]{2,1,0:T(8,128)(2,1)S(1)}, bf16[2,256,256]{2,1,0:T(8,128)(2,1)}, u32[]{:S(2)}) copy-start(bf16[2,256,256]{2,1,0:T(8,128)(2,1)} %constant.36.clone.t2) | copy-start | bytes 786436
  146.7 2.7 %copy-start.4 = (f32[2,128,128]{2,1,0:T(8,128)S(1)}, f32[2,128,128]{2,1,0:T(8,128)}, u32[]{:S(2)}) copy-start(f32[2,128,128]{2,1,0:T(8,128)} %constant.39.clone.turn) | copy-start | bytes 393220
  146.7 2.7 %copy-start.5 = (bf16[2,128,256]{2,1,0:T(8,128)(2,1)S(1)}, bf16[2,128,256]{2,1,0:T(8,128)(2,1)}, u32[]{:S(2)}) copy-start(bf16[2,128,256]{2,1,0:T(8,128)(2,1)} %constant.38.clone.t4) | copy-start | bytes 393220
  146.7 2.7 %copy-start.6 = (bf16[2,256,128]{2,1,0:T(8,128)(2,1)S(1)}, bf16[2,256,128]{2,1,0:T(8,128)(2,1)}, u32[]{:S(2)}) copy-start(bf16[2,256,128]{2,1,0:T(8,128)(2,1)} %constant.35.clone.t1) | copy-start | bytes 393220
  179.7 1.9 copy-start
  181.7 0.7 copy-start.1

commit v2 on v1

v2 whole, which is shorter than its diff:
```python
import functools
import math

import jax
import jax.numpy as jnp
import ml_dtypes
import numpy as np
from jax import lax
from jax.experimental import pallas as pl
from jax.experimental.pallas import tpu as pltpu
from jax.sharding import PartitionSpec as P

PIX = 256
LANES = 128
MIB = 1 << 20


def split(value):
    high = value.astype(jnp.bfloat16)
    return high, (value - high.astype(jnp.float32)).astype(jnp.bfloat16)


def product(left, right):
    dot = functools.partial(jnp.dot, preferred_element_type=jnp.float32)
    return dot(left[0], right[0]) + (dot(left[0], right[1]) + dot(left[1], right[0]))


def halves(table):
    high = table.astype(ml_dtypes.bfloat16)
    low = (table - high.astype(np.float64)).astype(ml_dtypes.bfloat16)
    return np.stack([high, low])


def transform_tables(side):
    index = np.arange(side)
    angle = (np.outer(index, index) % side) * (2.0 * math.pi / side)
    cos, sin = np.cos(angle), np.sin(angle)
    packed = np.stack([cos[: side // 2], -sin[: side // 2]], 1).reshape(side, side)
    packed[1] = cos[side // 2]
    twist = np.outer(np.arange(side // 2 + 1), index) * (2.0 * math.pi / (side * side))
    turn = np.stack([np.cos(twist), np.sin(twist)]).astype(np.float32)
    per_row = PIX // side
    last = packed.T / (side * side)
    last = last.reshape(side // per_row, per_row, side).swapaxes(0, 1).reshape(side, side)
    return (
        halves(packed),
        halves(np.block([[cos, -sin], [sin, cos]])),
        halves(np.block([[cos, sin], [-sin, cos]])),
        np.eye(side)[::-1].astype(ml_dtypes.bfloat16),
        turn,
        halves(last),
    )


def correct_kernel(
    plane, planes, x_ref, gain_ref, noise_ref, weight_ref, pattern_ref, t1, t2, t3, flip, turn, out_ref,
    cube, cal, slab, part, from_left, from_right, land, fold,
    raw_send, raw_recv, right_send, right_recv, left_send, left_recv, back_send, back_recv,
):
    me = lax.axis_index("det")
    z, q = me // plane, me % plane
    dets, samples = x_ref.shape
    side = t1.shape[1]
    chunks = side // plane
    hop = 2
    lag = hop * (planes - 1)
    mid_lag = max(lag + 2, 8)

    barrier = pltpu.get_barrier_semaphore()

    def partner(step):
        return lax.rem(q + step, plane)

    for step in range(1, plane):
        pl.semaphore_signal(barrier, inc=1, device_id={"det": z * plane + partner(step)})

    @pl.when(z > 0)
    def _():
        pl.semaphore_signal(barrier, inc=1, device_id={"det": me - plane})

    @pl.when(z < planes - 1)
    def _():
        pl.semaphore_signal(barrier, inc=1, device_id={"det": me + plane})

    def column(row):
        return pl.ds(pl.multiple_of(row * side, side), side)

    def spread(row):
        return pl.ds(row, dets, stride=side)

    def own_rows(owner):
        return pl.ds(pl.multiple_of(owner * dets, 8), dets)

    def raw_copy(chunk, step):
        other = partner(step)
        return pltpu.make_async_remote_copy(
            src_ref=cal.at[:, column(other * chunks + chunk)],
            dst_ref=slab.at[chunk, own_rows(q), :],
            send_sem=raw_send.at[chunk, step - 1],
            recv_sem=raw_recv.at[chunk, step - 1],
            device_id={"det": z * plane + other},
        )

    def back_copy(chunk, step):
        other = partner(step)
        return pltpu.make_async_remote_copy(
            src_ref=slab.at[chunk, own_rows(other), :],
            dst_ref=land.at[:, column(q * chunks + chunk)],
            send_sem=back_send.at[chunk, step - 1],
            recv_sem=back_recv.at[chunk, step - 1],
            device_id={"det": z * plane + other},
        )

    def right_copy(chunk):
        return pltpu.make_async_remote_copy(
            src_ref=from_left.at[chunk, 1],
            dst_ref=from_left.at[chunk, 0],
            send_sem=right_send.at[chunk],
            recv_sem=right_recv.at[chunk],
            device_id={"det": lax.rem(me + plane, plane * planes)},
        )

    def left_copy(chunk):
        return pltpu.make_async_remote_copy(
            src_ref=from_right.at[chunk, 1],
            dst_ref=from_right.at[chunk, 0],
            send_sem=left_send.at[chunk],
            recv_sem=left_recv.at[chunk],
            device_id={"det": lax.rem(me + plane * (planes - 1), plane * planes)},
        )

    gain = gain_ref[...]

    def to_cube(row, carry):
        cube[spread(row), :] = x_ref[:, column(row)] / gain
        return carry

    lax.fori_loop(0, side, to_cube, 0, unroll=4)
    first_table = (t1[0], t1[1])
    group = 8

    def first_stage(at, carry):
        rows = [pl.ds(pl.multiple_of((at * group + d) * side, side), side) for d in range(group)]
        section = product(first_table, split(jnp.concatenate([cube[row, :] for row in rows], axis=1)))
        for d in range(group):
            cube[rows[d], :] = section[:, d * side:(d + 1) * side]
        return carry

    lax.fori_loop(0, dets // group, first_stage, 0)
    at_ends = (z == 0).astype(jnp.int32) + (z == planes - 1).astype(jnp.int32)
    pl.semaphore_wait(barrier, plane + 1 - at_ends)

    def send_raw(chunk, carry):
        for owner in range(plane):
            row = owner * chunks + chunk
            cal[:, column(row)] = cube[spread(row), :]
        for step in range(1, plane):
            raw_copy(chunk, step).start()
        slab[chunk, own_rows(q), :] = cal[:, column(q * chunks + chunk)]
        return carry

    lax.fori_loop(0, chunks, send_raw, 0)
    weight = split(weight_ref[...])
    pattern = split(pattern_ref[...])

    def middle(real, imag, slots):
        turned = []
        for r, m, k in zip(real, imag, slots):
            cos, sin = turn[0, pl.ds(k, 1), :], turn[1, pl.ds(k, 1), :]
            turned.append(jnp.concatenate([r * cos + m * sin, m * cos - r * sin], axis=1))
        freq = product(split(jnp.concatenate(turned, axis=0)), (t2[0], t2[1]))
        weighted = []
        for at, k in enumerate(slots):
            noise = fold[own_rows(k), :]
            weighted.append(freq[at * dets:(at + 1) * dets] * jnp.concatenate([noise, noise], axis=1))
        section = product(split(jnp.concatenate(weighted, axis=0)), (t3[0], t3[1]))
        result = []
        for at, k in enumerate(slots):
            cos, sin = turn[0, pl.ds(k, 1), :], turn[1, pl.ds(k, 1), :]
            r, m = section[at * dets:(at + 1) * dets, :side], section[at * dets:(at + 1) * dets, side:]
            result.append((r * cos - m * sin, m * cos + r * sin))
        return result

    def one_step(i, carry):
        @pl.when(i < chunks)
        def _():
            for step in range(1, plane):
                raw_copy(i, step).wait_recv()
            part[i] = product(weight, split(slab[i]))

        c_right = i - hop * z

        @pl.when((c_right >= 0) & (c_right < chunks))
        def _():
            @pl.when(z == 0)
            def _():
                from_left[c_right, 1] = part[c_right]

            @pl.when(z > 0)
            def _():
                right_copy(c_right).wait_recv()
                from_left[c_right, 1] = part[c_right] + from_left[c_right, 0]

            @pl.when(z < planes - 1)
            def _():
                right_copy(c_right).start()

        c_left = i - hop * (planes - 1 - z)

        @pl.when((c_left >= 0) & (c_left < chunks))
        def _():
            @pl.when(z == planes - 1)
            def _():
                from_right[c_left, 1] = part[c_left]

            @pl.when(z < planes - 1)
            def _():
                left_copy(c_left).wait_recv()
                from_right[c_left, 1] = part[c_left] + from_right[c_left, 0]

            @pl.when(z > 0)
            def _():
                left_copy(c_left).start()

        c = i - lag

        @pl.when((c >= 0) & (c < chunks))
        def _():
            coeff = from_left[c, 1] + (from_right[c, 1] - part[c])
            slab[c] = slab[c] - product(pattern, split(coeff))
            for step in range(1, plane):
                back_copy(c, step).start()
            land[:, column(q * chunks + c)] = slab[c, own_rows(q), :]

        @pl.when(i < 4)
        def _():
            def regroup(at, carry):
                row = i * (side // 4) + at
                cube[spread(row), :] = noise_ref[:, column(row)]
                return carry

            lax.fori_loop(0, side // 4, regroup, 0, unroll=4)

        @pl.when((i >= 4) & (i < 8))
        def _():
            def swap(at, carry):
                det = (i - 4) * (dets // 4) + at
                fold[pl.ds(det, side, stride=dets), :] = cube[column(det), :].T
                return carry

            lax.fori_loop(0, dets // 4, swap, 0)

        @pl.when(i == 8)
        def _():
            def add_mirror(k, carry):
                high, low = split(fold[own_rows(side - k), :])
                dot = functools.partial(jnp.dot, preferred_element_type=jnp.float32)
                fold[own_rows(k), :] += dot(high, flip[...]) + dot(low, flip[...])
                return carry

            lax.fori_loop(1, side // 2, add_mirror, 0)

        pair = (i - mid_lag - 1) // 2

        @pl.when((i > mid_lag) & ((i - mid_lag) % 2 == 1) & (pair < chunks // 2))
        def _():
            for step in range(1, plane):
                back_copy(2 * pair, step).wait_recv()
                back_copy(2 * pair + 1, step).wait_recv()
            slots = [owner * (chunks // 2) + pair for owner in range(plane)]
            real = [land[:, column(2 * k)] for k in slots]
            imag = [land[:, column(2 * k + 1)] for k in slots]
            for k, (r, m) in zip(slots, middle(real, imag, slots)):
                out_ref[spread(2 * k), :] = r
                out_ref[spread(2 * k + 1), :] = m

            @pl.when(pair == 0)
            def _():
                none = jnp.zeros((dets, side), jnp.float32)
                ends = middle([real[0], imag[0]], [none, none], [0, side // 2])
                out_ref[spread(0), :] = ends[0][0]
                out_ref[spread(1), :] = ends[1][0]

        return carry

    lax.fori_loop(0, chunks + mid_lag + 1, one_step, 0)

    def finish(chunk, carry):
        for step in range(1, plane):
            back_copy(chunk, step).wait_send()
            raw_copy(chunk, step).wait_send()

        @pl.when(z < planes - 1)
        def _():
            right_copy(chunk).wait_send()

        @pl.when(z > 0)
        def _():
            left_copy(chunk).wait_send()

        return carry

    lax.fori_loop(0, chunks, finish, 0)


def correct(stream, gains, noise, mode_pattern, mode_weights, tables, size):
    dets, samples = stream.shape
    rank = mode_pattern.shape[1]
    side = math.isqrt(samples)
    plane = 4 if size % 4 == 0 else 1
    planes = size // plane
    chunks = side // plane
    rows = plane * dets
    start = (lax.axis_index("det") // plane) * rows
    weights = lax.dynamic_slice_in_dim(mode_weights, start, rows, 0).T
    pattern = lax.dynamic_slice_in_dim(mode_pattern, start, rows, 0)
    f32 = jnp.float32
    sem = pltpu.SemaphoreType.DMA
    coeffs = pltpu.VMEM((chunks, rank, side), f32)
    chain = pltpu.VMEM((chunks, 2, rank, side), f32)
    whole = pltpu.VMEM((dets, samples), f32)
    cube = pltpu.VMEM((dets * side, side), f32)
    return pl.pallas_call(
        functools.partial(correct_kernel, plane, planes),
        out_shape=jax.ShapeDtypeStruct((dets * side, side), f32),
        in_specs=[pl.BlockSpec(memory_space=pltpu.VMEM)] * (5 + len(tables)),
        out_specs=pl.BlockSpec(memory_space=pltpu.VMEM),
        scratch_shapes=[
            cube, whole, pltpu.VMEM((chunks, rows, side), f32), coeffs, chain, chain, whole, cube,
            sem((chunks, plane)), sem((chunks, plane)), sem((chunks,)), sem((chunks,)),
            sem((chunks,)), sem((chunks,)), sem((chunks, plane)), sem((chunks, plane)),
        ],
        compiler_params=pltpu.CompilerParams(
            collective_id=0, has_side_effects=True, vmem_limit_bytes=60 * MIB
        ),
        name="correct",
    )(stream, gains.reshape(dets, 1), noise, weights, pattern, *tables)


def bin_kernel(x_ref, row_ref, hit_ref, t4, out_ref, acc_ref, count_ref, rows_ref):
    batch, side, _ = x_ref.shape
    per_row = PIX // side
    tiles = side // per_row
    packed = jnp.concatenate([x_ref[b] for b in range(batch)], axis=1)
    result = product((t4[0], t4[1]), split(packed))
    tiled = []
    for b in range(batch):
        part = result[:, b * side:(b + 1) * side]
        rows_ref[pl.ds(b * side, side), :] = part
        tiled.append(jnp.concatenate([part[p * tiles:(p + 1) * tiles] for p in range(per_row)], axis=1))
    for tile in range(tiles):
        for p in range(per_row):
            at = (tile * per_row + p) * side
            out_ref[:, at:at + side] = rows_ref[pl.ds(p * tiles + tile, batch, stride=side), :]
    high, low = split(jnp.concatenate(tiled, axis=0))
    blocks = acc_ref.shape[0]
    ladder = lax.broadcasted_iota(jnp.int32, (blocks, batch * tiles), 0)
    table = jnp.where(row_ref[...] == ladder, hit_ref[...], 0.0).astype(jnp.bfloat16)
    dot = functools.partial(jnp.dot, preferred_element_type=jnp.float32)
    ones = jnp.ones((8, batch * tiles), jnp.bfloat16)
    counts = lax.dot_general(ones, table, (((1,), (1,)), ((), ())), preferred_element_type=jnp.float32)

    @pl.when(pl.program_id(0) == 0)
    def _():
        acc_ref[...] = jnp.zeros_like(acc_ref)
        count_ref[...] = jnp.zeros_like(count_ref)

    acc_ref[...] += dot(table, high) + dot(table, low)
    count_ref[...] += counts[:1]


def finish_and_bin(packed, rows, hits, table, blocks):
    dets, side, _ = packed.shape
    batch = 8
    tiles = side * side // PIX
    line = pl.BlockSpec((1, batch * tiles), lambda i: (0, i))
    return pl.pallas_call(
        bin_kernel,
        grid=(dets // batch,),
        out_shape=(
            jax.ShapeDtypeStruct((dets, side * side), jnp.float32),
            jax.ShapeDtypeStruct((blocks, PIX), jnp.float32),
            jax.ShapeDtypeStruct((1, blocks), jnp.float32),
        ),
        in_specs=[
            pl.BlockSpec((batch, side, side), lambda i: (i, 0, 0)),
            line,
            line,
            pl.BlockSpec(table.shape, lambda i: (0, 0, 0)),
        ],
        out_specs=(
            pl.BlockSpec((batch, side * side), lambda i: (i, 0)),
            pl.BlockSpec((blocks, PIX), lambda i: (0, 0)),
            pl.BlockSpec((1, blocks), lambda i: (0, 0)),
        ),
        scratch_shapes=[pltpu.VMEM((batch * side, side), jnp.float32)],
        compiler_params=pltpu.CompilerParams(vmem_limit_bytes=48 * MIB),
        name="finish_and_bin",
    )(packed, rows, hits, table)


def map_kernel(size, acc_ref, count_ref, out_ref, landed, tallies, send_sem, recv_sem, tally_send, tally_recv):
    me = lax.axis_index("det")
    rows = out_ref.shape[0]
    barrier = pltpu.get_barrier_semaphore()

    def greet(step, carry):
        pl.semaphore_signal(barrier, inc=1, device_id={"det": lax.rem(me + step, size)})
        return carry

    lax.fori_loop(1, size, greet, 0)
    pl.semaphore_wait(barrier, size - 1)

    def copy(step):
        other = lax.rem(me + step, size)
        return pltpu.make_async_remote_copy(
            src_ref=acc_ref.at[pl.ds(pl.multiple_of(other * rows, 8), rows), :],
            dst_ref=landed.at[step],
            send_sem=send_sem.at[step],
            recv_sem=recv_sem.at[step],
            device_id={"det": other},
        )

    def tally(step):
        return pltpu.make_async_remote_copy(
            src_ref=count_ref,
            dst_ref=tallies.at[step],
            send_sem=tally_send.at[step],
            recv_sem=tally_recv.at[step],
            device_id={"det": lax.rem(me + step, size)},
        )

    def start(step, carry):
        copy(step).start()
        tally(step).start()
        return carry

    lax.fori_loop(1, size, start, 0)

    def add(step, total):
        copy(step).wait_recv()
        tally(step).wait_recv()
        return total[0] + landed[step], total[1] + tallies[step]

    own = acc_ref[pl.ds(pl.multiple_of(me * rows, 8), rows), :]
    sums, counts = lax.fori_loop(1, size, add, (own, count_ref[...]))
    shape = (rows, counts.shape[1])
    mine = lax.broadcasted_iota(jnp.int32, shape, 1) == lax.broadcasted_iota(jnp.int32, shape, 0) + me * rows
    counts = jnp.sum(jnp.where(mine, counts, 0.0), axis=1, keepdims=True)
    out_ref[...] = sums / jnp.sqrt(1.0 + counts)

    def finish(step, carry):
        copy(step).wait_send()
        tally(step).wait_send()
        return carry

    lax.fori_loop(1, size, finish, 0)


def combine_map(acc, counts, size):
    blocks, columns = acc.shape
    rows = blocks // size
    sem = pltpu.SemaphoreType.DMA((size,))
    return pl.pallas_call(
        functools.partial(map_kernel, size),
        out_shape=jax.ShapeDtypeStruct((rows, columns), jnp.float32),
        in_specs=[pl.BlockSpec(memory_space=pltpu.VMEM)] * 2,
        out_specs=pl.BlockSpec(memory_space=pltpu.VMEM),
        scratch_shapes=[
            pltpu.VMEM((size, rows, columns), jnp.float32),
            pltpu.VMEM((size, 1, blocks), jnp.float32),
            sem, sem, sem, sem,
        ],
        compiler_params=pltpu.CompilerParams(collective_id=1, has_side_effects=True),
        name="combine_map",
    )(acc, counts)


def shards(size, timestream, gains, mode_pattern, mode_weights, noise_weight, block_ids, hits, sky_rows):
    items, dets, samples = timestream.shape
    side = math.isqrt(samples)
    ids_flat = block_ids.reshape(-1)
    blocks = sky_rows.shape[0]
    ladder = lax.broadcasted_iota(jnp.int32, (blocks, ids_flat.shape[0]), 0)
    rows = jnp.sum(jnp.where(ids_flat[None, :] == ladder, sky_rows[:, None], 0), axis=0)
    weight = hits.reshape(1, -1).astype(jnp.float32)
    *tables, last = [jnp.asarray(table) for table in transform_tables(side)]
    packed = correct(
        timestream.reshape(items * dets, samples), gains.reshape(-1), noise_weight, mode_pattern, mode_weights,
        tables, size,
    )
    filtered, acc, counts = finish_and_bin(packed.reshape(dets, side, side), rows[None, :], weight, last, blocks)
    return (filtered.reshape(items, dets, samples), combine_map(acc, counts, size))


def solution(mesh):
    in_specs = (
        P("grp", "det", None),
        P("grp", "det"),
        P("grp", None),
        P("grp", None),
        P(("grp", "det"), None),
        P("grp", "det", None),
        P("grp", "det", None),
        P("grp"),
    )
    out_specs = (P("grp", "det", None), P(("grp", "det"), None))
    body = functools.partial(shards, mesh.shape["det"])
    return jax.shard_map(body, mesh=mesh, in_specs=in_specs, out_specs=out_specs, check_vma=False)
```

time: 202 us -> 187 us (0.926); the launches traced: 198 us -> 187 us
  local copies, waits for them, and re-layouts: 21.6 us -> 9.63 us
    unnamed x20 -> x10, local copies, waits for them, and re-layouts: 12.6 us -> 5.59 us
    reshape x1 -> x0, local copies, waits for them, and re-layouts: 4.94 us -> none  [shards(): return (filtered.reshape(items, dets, samples), combine_map(acc, size))]
where the time goes in v2:
time: 187 us
  Pallas kernels  174 us (93%)
  local copies, waits for them, and re-layouts  9.63 us (5%)
  other arithmetic  2.18 us (1%)
    pallas_call x1, Pallas kernels, correct(): pl.pallas_call(functools.partial(correct_kernel, plane, planes), out_shap...  154 us
    pallas_call x1, Pallas kernels, combine_map(): pl.pallas_call(functools.partial(map_kernel, size), out_shape=jax.ShapeDt...  11 us
    pallas_call x1, Pallas kernels, finish_and_bin(): pl.pallas_call(bin_kernel, grid=(dets // batch,), out_shape=(jax.ShapeDty...  8.83 us
    unnamed x10, local copies, waits for them, and re-layouts  5.59 us

profile of v2, /device:TPU:0, one launch (start us, length us, event | category | flops | bytes accessed | tf_op | source)
XLA Modules:
  0.0 186.6 jit_solution(14509924998190558698)
XLA Ops:
  0.6 0.8 eq.10
  1.5 1.4 select_reduce_fusion
  2.9 1.3 copy.19.gain_ref
  4.3 0.8 convert_element_type.5
  5.0 0.1 convert_element_type.6.hit_ref
  5.1 1.8 constant_dynamic-slice_fusion
  6.9 0.8 copy.20
  7.7 0.0 copy-start.2
  7.7 154.3 %correct.1 = f32[8192,128]{1,0:T(8,128)} custom-call(f32[64,16384]{1,0:T(8,128)} %bitcast.8, f32[64,1]{1,0:T(8,128)} %copy.19.gain_ref, f32[64,16384]{1,0:T(8,128)} %noise_ref.1, f32[256,256]{1,0:T(8,128)} %bitcast.9, f32[256,256]{1,0:T(8,128)} %get-tuple-element.8.pattern_ref, bf16[2,128,128]{2,1,0:T(8,128)(2,1)} %constant.37.clone.t1, ...), custom_call_target="tpu_custom_call" | custom-call | tf_op jit(solution)/shard_map/correct/pallas_call | solution.py:323
  162.0 0.0 copy-done.2
  162.0 0.0 copy-start
  162.0 2.2 %copy-done = f32[8192,128]{1,0:T(8,128)S(1)} copy-done((f32[8192,128]{1,0:T(8,128)S(1)}, f32[8192,128]{1,0:T(8,128)}, u32[]{:S(2)}) %copy-start) | copy-done | bytes 4194328
  164.2 8.8 %finish_and_bin.1 = (f32[64,16384]{1,0:T(8,128)}, f32[256,256]{1,0:T(8,128)S(1)}, f32[1,256]{1,0:T(1,128)S(1)}) custom-call(f32[64,128,128]{2,1,0:T(8,128)S(1)} %bitcast.6, s32[1,4096]{1,0:T(1,128)S(1)} %bitcast.7, f32[1,4096]{1,0:T(1,128)S(1)} %convert_element_type.6.hit_ref, bf16[2,128,128]{2,1,0:T(8,128)(2,1)S(1)} %copy-done.2), custom_call_target="tpu_custom_call" | custom-call | tf_op jit(solution)/shard_map/finish_and_bin/pallas_call | solution.py:377
  173.0 0.0 copy-start.1
  173.0 0.7 copy-done.1
  173.7 0.0 copy-start.3
  173.7 0.6 copy-done.3
  174.3 11.0 %combine_map.1 = f32[16,256]{1,0:T(8,128)} custom-call(f32[256,256]{1,0:T(8,128)} %copy-done.1, f32[1,256]{1,0:T(1,128)} %copy-done.3), custom_call_target="tpu_custom_call" | custom-call | tf_op jit(solution)/shard_map/combine_map/pallas_call | solution.py:464
  185.3 1.3 copy.22
Async XLA Ops:
  7.7 154.3 %copy-start.2 = (bf16[2,128,128]{2,1,0:T(8,128)(2,1)S(1)}, bf16[2,128,128]{2,1,0:T(8,128)(2,1)}, u32[]{:S(2)}) copy-start(bf16[2,128,128]{2,1,0:T(8,128)(2,1)} %constant.42.clone.t4) | copy-start | bytes 196612
  162.0 2.2 %copy-start = (f32[8192,128]{1,0:T(8,128)S(1)}, f32[8192,128]{1,0:T(8,128)}, u32[]{:S(2)}) copy-start(f32[8192,128]{1,0:T(8,128)} %correct.1) | copy-start | bytes 12582916
  173.0 0.7 copy-start.1
  173.7 0.6 copy-start.3

commit v3 on v2

--- a/solution.py
+++ b/solution.py
@@ -53,8 +53,8 @@
 
 
 def correct_kernel(
-    plane, planes, x_ref, gain_ref, noise_ref, weight_ref, pattern_ref, t1, t2, t3, flip, turn, out_ref,
-    cube, cal, slab, part, from_left, from_right, land, fold,
+    plane, planes, x_ref, gain_ref, noise_hbm, weight_ref, pattern_ref, t1, t2, t3, flip, turn, out_ref,
+    noise_ref, noise_sem, cube, cal, slab, part, from_left, from_right, land, fold,
     raw_send, raw_recv, right_send, right_recv, left_send, left_recv, back_send, back_recv,
 ):
     me = lax.axis_index("det")
@@ -65,6 +65,9 @@
     hop = 2
     lag = hop * (planes - 1)
     mid_lag = max(lag + 2, 8)
+    lead = min(4, chunks)
+    noise_copy = pltpu.make_async_copy(noise_hbm, noise_ref, noise_sem)
+    noise_copy.start()
 
     barrier = pltpu.get_barrier_semaphore()
 
@@ -129,10 +132,13 @@
             device_id={"det": lax.rem(me + plane * (planes - 1), plane * planes)},
         )
 
-    gain = gain_ref[...]
+    shape = (dets, dets)
+    diagonal = lax.broadcasted_iota(jnp.int32, shape, 0) == lax.broadcasted_iota(jnp.int32, shape, 1)
+    gain = jnp.sum(jnp.where(diagonal, gain_ref[...], 0.0), axis=1, keepdims=True)
+    scale = jnp.broadcast_to(1.0 / gain, (dets, side))
 
     def to_cube(row, carry):
-        cube[spread(row), :] = x_ref[:, column(row)] / gain
+        cube[spread(row), :] = x_ref[:, column(row)] * scale
         return carry
 
     lax.fori_loop(0, side, to_cube, 0, unroll=4)
@@ -159,9 +165,10 @@
         slab[chunk, own_rows(q), :] = cal[:, column(q * chunks + chunk)]
         return carry
 
-    lax.fori_loop(0, chunks, send_raw, 0)
-    weight = split(weight_ref[...])
-    pattern = split(pattern_ref[...])
+    lax.fori_loop(0, lead, send_raw, 0)
+    in_plane = pl.ds(pl.multiple_of(z * plane * dets, 8), plane * dets)
+    weight = split(weight_ref[in_plane, :].T)
+    pattern = split(pattern_ref[in_plane, :])
 
     def middle(real, imag, slots):
         turned = []
@@ -222,6 +229,10 @@
             def _():
                 left_copy(c_left).start()
 
+        @pl.when(i + lead < chunks)
+        def _():
+            send_raw(i + lead, 0)
+
         c = i - lag
 
         @pl.when((c >= 0) & (c < chunks))
@@ -232,11 +243,15 @@
                 back_copy(c, step).start()
             land[:, column(q * chunks + c)] = slab[c, own_rows(q), :]
 
+        @pl.when(i == 0)
+        def _():
+            noise_copy.wait()
+
         @pl.when(i < 4)
         def _():
             def regroup(at, carry):
                 row = i * (side // 4) + at
-                cube[spread(row), :] = noise_ref[:, column(row)]
+                out_ref[spread(row), :] = noise_ref[:, column(row)]
                 return carry
 
             lax.fori_loop(0, side // 4, regroup, 0, unroll=4)
@@ -245,7 +260,7 @@
         def _():
             def swap(at, carry):
                 det = (i - 4) * (dets // 4) + at
-                fold[pl.ds(det, side, stride=dets), :] = cube[column(det), :].T
+                fold[pl.ds(det, side, stride=dets), :] = out_ref[column(det), :].T
                 return carry
 
             lax.fori_loop(0, dets // 4, swap, 0)
@@ -311,10 +326,8 @@
     planes = size // plane
     chunks = side // plane
     rows = plane * dets
-    start = (lax.axis_index("det") // plane) * rows
-    weights = lax.dynamic_slice_in_dim(mode_weights, start, rows, 0).T
-    pattern = lax.dynamic_slice_in_dim(mode_pattern, start, rows, 0)
     f32 = jnp.float32
+    vmem = pl.BlockSpec(memory_space=pltpu.VMEM)
     sem = pltpu.SemaphoreType.DMA
     coeffs = pltpu.VMEM((chunks, rank, side), f32)
     chain = pltpu.VMEM((chunks, 2, rank, side), f32)
@@ -323,10 +336,10 @@
     return pl.pallas_call(
         functools.partial(correct_kernel, plane, planes),
         out_shape=jax.ShapeDtypeStruct((dets * side, side), f32),
-        in_specs=[pl.BlockSpec(memory_space=pltpu.VMEM)] * (5 + len(tables)),
+        in_specs=[vmem, vmem, pl.BlockSpec(memory_space=pl.ANY)] + [vmem] * (2 + len(tables)),
         out_specs=pl.BlockSpec(memory_space=pltpu.VMEM),
         scratch_shapes=[
-            cube, whole, pltpu.VMEM((chunks, rows, side), f32), coeffs, chain, chain, whole, cube,
+            whole, sem(()), cube, whole, pltpu.VMEM((chunks, rows, side), f32), coeffs, chain, chain, whole, cube,
             sem((chunks, plane)), sem((chunks, plane)), sem((chunks,)), sem((chunks,)),
             sem((chunks,)), sem((chunks,)), sem((chunks, plane)), sem((chunks, plane)),
         ],
@@ -334,10 +347,10 @@
             collective_id=0, has_side_effects=True, vmem_limit_bytes=60 * MIB
         ),
         name="correct",
-    )(stream, gains.reshape(dets, 1), noise, weights, pattern, *tables)
-
-
-def bin_kernel(x_ref, row_ref, hit_ref, t4, out_ref, acc_ref, count_ref, rows_ref):
+    )(stream, gains, noise, mode_weights, mode_pattern, *tables)
+
+
+def bin_kernel(x_ref, id_ref, hit_ref, sky_ref, t4, out_ref, acc_ref, count_ref, rows_ref):
     batch, side, _ = x_ref.shape
     per_row = PIX // side
     tiles = side // per_row
@@ -355,7 +368,9 @@
     high, low = split(jnp.concatenate(tiled, axis=0))
     blocks = acc_ref.shape[0]
     ladder = lax.broadcasted_iota(jnp.int32, (blocks, batch * tiles), 0)
-    table = jnp.where(row_ref[...] == ladder, hit_ref[...], 0.0).astype(jnp.bfloat16)
+    ids = jnp.concatenate([id_ref[b:b + 1, :] for b in range(batch)], axis=1)
+    hits = jnp.concatenate([hit_ref[b:b + 1, :] for b in range(batch)], axis=1).astype(jnp.float32)
+    table = jnp.where(ids == ladder, hits, 0.0).astype(jnp.bfloat16)
     dot = functools.partial(jnp.dot, preferred_element_type=jnp.float32)
     ones = jnp.ones((8, batch * tiles), jnp.bfloat16)
     counts = lax.dot_general(ones, table, (((1,), (1,)), ((), ())), preferred_element_type=jnp.float32)
@@ -368,12 +383,28 @@
     acc_ref[...] += dot(table, high) + dot(table, low)
     count_ref[...] += counts[:1]
 
-
-def finish_and_bin(packed, rows, hits, table, blocks):
+    @pl.when(pl.program_id(0) == pl.num_programs(0) - 1)
+    def _():
+        ladder = lax.broadcasted_iota(jnp.int32, (blocks, blocks), 0)
+        place = jnp.where(sky_ref[...] == ladder, 1.0, 0.0).astype(jnp.bfloat16)
+        total = acc_ref[...]
+        high, low = split(total)
+        rest = (total - high.astype(jnp.float32) - low.astype(jnp.float32)).astype(jnp.bfloat16)
+        acc_ref[...] = dot(place, high) + (dot(place, low) + dot(place, rest))
+        tally = jnp.broadcast_to(count_ref[...], (8, blocks))
+        across = functools.partial(
+            lax.dot_general, dimension_numbers=(((1,), (1,)), ((), ())), preferred_element_type=jnp.float32
+        )
+        high, low = split(tally)
+        count_ref[...] = (across(high, place) + across(low, place))[:1]
+
+
+def finish_and_bin(packed, ids, hits, sky_rows, table):
     dets, side, _ = packed.shape
     batch = 8
     tiles = side * side // PIX
-    line = pl.BlockSpec((1, batch * tiles), lambda i: (0, i))
+    blocks = sky_rows.shape[1]
+    line = pl.BlockSpec((batch, tiles), lambda i: (i, 0))
     return pl.pallas_call(
         bin_kernel,
         grid=(dets // batch,),
@@ -386,6 +417,7 @@
             pl.BlockSpec((batch, side, side), lambda i: (i, 0, 0)),
             line,
             line,
+            pl.BlockSpec((1, blocks), lambda i: (0, 0)),
             pl.BlockSpec(table.shape, lambda i: (0, 0, 0)),
         ],
         out_specs=(
@@ -394,9 +426,9 @@
             pl.BlockSpec((1, blocks), lambda i: (0, 0)),
         ),
         scratch_shapes=[pltpu.VMEM((batch * side, side), jnp.float32)],
-        compiler_params=pltpu.CompilerParams(vmem_limit_bytes=48 * MIB),
+        compiler_params=pltpu.CompilerParams(vmem_limit_bytes=60 * MIB),
         name="finish_and_bin",
-    )(packed, rows, hits, table)
+    )(packed, ids, hits, sky_rows, table)
 
 
 def map_kernel(size, acc_ref, count_ref, out_ref, landed, tallies, send_sem, recv_sem, tally_send, tally_recv):
@@ -479,17 +511,14 @@
 def shards(size, timestream, gains, mode_pattern, mode_weights, noise_weight, block_ids, hits, sky_rows):
     items, dets, samples = timestream.shape
     side = math.isqrt(samples)
-    ids_flat = block_ids.reshape(-1)
-    blocks = sky_rows.shape[0]
-    ladder = lax.broadcasted_iota(jnp.int32, (blocks, ids_flat.shape[0]), 0)
-    rows = jnp.sum(jnp.where(ids_flat[None, :] == ladder, sky_rows[:, None], 0), axis=0)
-    weight = hits.reshape(1, -1).astype(jnp.float32)
     *tables, last = [jnp.asarray(table) for table in transform_tables(side)]
     packed = correct(
-        timestream.reshape(items * dets, samples), gains.reshape(-1), noise_weight, mode_pattern, mode_weights,
+        timestream.reshape(items * dets, samples), gains, noise_weight, mode_pattern, mode_weights,
         tables, size,
     )
-    filtered, acc, counts = finish_and_bin(packed.reshape(dets, side, side), rows[None, :], weight, last, blocks)
+    filtered, acc, counts = finish_and_bin(
+        packed.reshape(dets, side, side), block_ids.reshape(dets, -1), hits.reshape(dets, -1), sky_rows[None, :], last
+    )
     return (filtered.reshape(items, dets, samples), combine_map(acc, counts, size))
 
 

time: 187 us -> 164 us (0.88)
  Pallas kernels: 174 us -> 161 us
  local copies, waits for them, and re-layouts: 9.63 us -> 1.32 us
  other arithmetic: 2.18 us -> 0 us
    pallas_call x1, Pallas kernels: 154 us -> 138 us  [correct(): pl.pallas_call(functools.partial(correct_kernel, plane, planes), out_shap...]
    unnamed x10 -> x1, local copies, waits for them, and re-layouts: 5.59 us -> 1.32 us
    pallas_call x1, Pallas kernels: 8.83 us -> 11.6 us  [finish_and_bin(): pl.pallas_call(bin_kernel, grid=(dets // batch,), out_shape=(jax.ShapeDty...]
where the time goes in v3:
time: 164 us; the launch traced here: 163 us
  Pallas kernels  161 us (98%)
    pallas_call x1, Pallas kernels, correct(): pl.pallas_call(functools.partial(correct_kernel, plane, planes), out_shap...  138 us
    pallas_call x1, Pallas kernels, combine_map(): pl.pallas_call(functools.partial(map_kernel, size), out_shape=jax.ShapeDt...  11.6 us
    pallas_call x1, Pallas kernels, finish_and_bin(): pl.pallas_call(bin_kernel, grid=(dets // batch,), out_shape=(jax.ShapeDty...  11.6 us

profile of v3, /device:TPU:0, one launch (start us, length us, event | category | flops | bytes accessed | tf_op | source)
XLA Modules:
  0.0 163.2 jit_solution(7951616746052421893)
XLA Ops:
  0.6 138.0 %correct.1 = f32[8192,128]{1,0:T(8,128)} custom-call(f32[64,16384]{1,0:T(8,128)} %bitcast.7, f32[1,64]{1,0:T(1,128)} %gain_ref.1, f32[64,16384]{1,0:T(8,128)} %noise_hbm.1, f32[1024,256]{1,0:T(8,128)} %weight_ref.1, f32[1024,256]{1,0:T(8,128)} %pattern_ref.1, bf16[2,128,128]{2,1,0:T(8,128)(2,1)} %constant.12.clone.t1, ...), custom_call_target="tpu_custom_call" | custom-call | tf_op jit(solution)/shard_map/correct/pallas_call | solution.py:336
  138.7 11.6 %finish_and_bin.1 = (f32[64,16384]{1,0:T(8,128)}, f32[256,256]{1,0:T(8,128)}, f32[1,256]{1,0:T(1,128)}) custom-call(f32[64,128,128]{2,1,0:T(8,128)} %bitcast.6, s32[64,64]{1,0:T(8,128)} %bitcast.8, s32[64,64]{1,0:T(8,128)} %bitcast.9, s32[1,256]{1,0:T(1,128)} %bitcast.10, bf16[2,128,128]{2,1,0:T(8,128)(2,1)} %constant.17.clone.t4), custom_call_target="tpu_custom_call" | custom-call | tf_op jit(solution)/shard_map/finish_and_bin/pallas_call | solution.py:408
  150.3 11.6 %combine_map.1 = f32[16,256]{1,0:T(8,128)} custom-call(f32[256,256]{1,0:T(8,128)} %get-tuple-element.6.acc_ref, f32[1,256]{1,0:T(1,128)} %get-tuple-element.7.count_ref), custom_call_target="tpu_custom_call" | custom-call | tf_op jit(solution)/shard_map/combine_map/pallas_call | solution.py:496
  161.9 1.3 copy.17

commit v4 on v3

--- a/solution.py
+++ b/solution.py
@@ -61,11 +61,11 @@
     z, q = me // plane, me % plane
     dets, samples = x_ref.shape
     side = t1.shape[1]
-    chunks = side // plane
-    hop = 2
-    lag = hop * (planes - 1)
-    mid_lag = max(lag + 2, 8)
-    lead = min(4, chunks)
+    pairs = side // plane // 2
+    rank = part.shape[1]
+    lag = planes - 1
+    mid_lag = max(lag + 1, 4)
+    lead = min(3, pairs)
     noise_copy = pltpu.make_async_copy(noise_hbm, noise_ref, noise_sem)
     noise_copy.start()
 
@@ -88,47 +88,52 @@
     def column(row):
         return pl.ds(pl.multiple_of(row * side, side), side)
 
+    def slot(k):
+        return pl.ds(pl.multiple_of(k * 2 * side, 2 * side), 2 * side)
+
     def spread(row):
         return pl.ds(row, dets, stride=side)
 
     def own_rows(owner):
         return pl.ds(pl.multiple_of(owner * dets, 8), dets)
 
-    def raw_copy(chunk, step):
+    def raw_copy(pair, step):
         other = partner(step)
         return pltpu.make_async_remote_copy(
-            src_ref=cal.at[:, column(other * chunks + chunk)],
-            dst_ref=slab.at[chunk, own_rows(q), :],
-            send_sem=raw_send.at[chunk, step - 1],
-            recv_sem=raw_recv.at[chunk, step - 1],
+            src_ref=cal.at[:, slot(other * pairs + pair)],
+            dst_ref=slab.at[pair, own_rows(q), :],
+            send_sem=raw_send.at[pair, step - 1],
+            recv_sem=raw_recv.at[pair, step - 1],
             device_id={"det": z * plane + other},
         )
 
-    def back_copy(chunk, step):
+    def back_copy(pair, step):
         other = partner(step)
         return pltpu.make_async_remote_copy(
-            src_ref=slab.at[chunk, own_rows(other), :],
-            dst_ref=land.at[:, column(q * chunks + chunk)],
-            send_sem=back_send.at[chunk, step - 1],
-            recv_sem=back_recv.at[chunk, step - 1],
+            src_ref=slab.at[pair, own_rows(other), :],
+            dst_ref=land.at[:, slot(q * pairs + pair)],
+            send_sem=back_send.at[pair, step - 1],
+            recv_sem=back_recv.at[pair, step - 1],
             device_id={"det": z * plane + other},
         )
 
-    def right_copy(chunk):
+    halves_of = [pl.ds(h * (rank // 2), rank // 2) for h in range(2)]
+
+    def right_copy(pair, h):
         return pltpu.make_async_remote_copy(
-            src_ref=from_left.at[chunk, 1],
-            dst_ref=from_left.at[chunk, 0],
-            send_sem=right_send.at[chunk],
-            recv_sem=right_recv.at[chunk],
+            src_ref=from_left.at[pair, 1, halves_of[h], :],
+            dst_ref=from_left.at[pair, 0, halves_of[h], :],
+            send_sem=right_send.at[pair, h],
+            recv_sem=right_recv.at[pair, h],
             device_id={"det": lax.rem(me + plane, plane * planes)},
         )
 
-    def left_copy(chunk):
+    def left_copy(pair, h):
         return pltpu.make_async_remote_copy(
-            src_ref=from_right.at[chunk, 1],
-            dst_ref=from_right.at[chunk, 0],
-            send_sem=left_send.at[chunk],
-            recv_sem=left_recv.at[chunk],
+            src_ref=from_right.at[pair, 1, halves_of[h], :],
+            dst_ref=from_right.at[pair, 0, halves_of[h], :],
+            send_sem=left_send.at[pair, h],
+            recv_sem=left_recv.at[pair, h],
             device_id={"det": lax.rem(me + plane * (planes - 1), plane * planes)},
         )
 
@@ -141,7 +146,7 @@
         cube[spread(row), :] = x_ref[:, column(row)] * scale
         return carry
 
-    lax.fori_loop(0, side, to_cube, 0, unroll=4)
+    lax.fori_loop(0, side, to_cube, 0, unroll=8)
     first_table = (t1[0], t1[1])
     group = 8
 
@@ -156,19 +161,27 @@
     at_ends = (z == 0).astype(jnp.int32) + (z == planes - 1).astype(jnp.int32)
     pl.semaphore_wait(barrier, plane + 1 - at_ends)
 
-    def send_raw(chunk, carry):
+    def send_raw(pair, carry):
         for owner in range(plane):
-            row = owner * chunks + chunk
-            cal[:, column(row)] = cube[spread(row), :]
+            k = owner * pairs + pair
+            cal[:, column(2 * k)] = cube[spread(2 * k), :]
+            cal[:, column(2 * k + 1)] = cube[spread(2 * k + 1), :]
         for step in range(1, plane):
-            raw_copy(chunk, step).start()
-        slab[chunk, own_rows(q), :] = cal[:, column(q * chunks + chunk)]
+            raw_copy(pair, step).start()
+        slab[pair, own_rows(q), :] = cal[:, slot(q * pairs + pair)]
         return carry
 
     lax.fori_loop(0, lead, send_raw, 0)
     in_plane = pl.ds(pl.multiple_of(z * plane * dets, 8), plane * dets)
     weight = split(weight_ref[in_plane, :].T)
     pattern = split(pattern_ref[in_plane, :])
+
+    def measure_modes(pair):
+        for step in range(1, plane):
+            raw_copy(pair, step).wait_recv()
+        part[pair] = product(weight, split(slab[pair]))
+
+    measure_modes(0)
 
     def middle(real, imag, slots):
         turned = []
@@ -189,100 +202,101 @@
         return result
 
     def one_step(i, carry):
-        @pl.when(i < chunks)
-        def _():
-            for step in range(1, plane):
-                raw_copy(i, step).wait_recv()
-            part[i] = product(weight, split(slab[i]))
-
-        c_right = i - hop * z
-
-        @pl.when((c_right >= 0) & (c_right < chunks))
-        def _():
-            @pl.when(z == 0)
+        c_right = i - z
+        c_left = i - (planes - 1 - z)
+        for h in range(2):
+            rows = halves_of[h]
+
+            @pl.when((c_right >= 0) & (c_right < pairs))
             def _():
-                from_left[c_right, 1] = part[c_right]
-
-            @pl.when(z > 0)
+                @pl.when(z == 0)
+                def _():
+                    from_left[c_right, 1, rows, :] = part[c_right, rows, :]
+
+                @pl.when(z > 0)
+                def _():
+                    right_copy(c_right, h).wait_recv()
+                    from_left[c_right, 1, rows, :] = part[c_right, rows, :] + from_left[c_right, 0, rows, :]
+
+                @pl.when(z < planes - 1)
+                def _():
+                    right_copy(c_right, h).start()
+
+            @pl.when((c_left >= 0) & (c_left < pairs))
             def _():
-                right_copy(c_right).wait_recv()
-                from_left[c_right, 1] = part[c_right] + from_left[c_right, 0]
-
-            @pl.when(z < planes - 1)
-            def _():
-                right_copy(c_right).start()
-
-        c_left = i - hop * (planes - 1 - z)
-
-        @pl.when((c_left >= 0) & (c_left < chunks))
-        def _():
-            @pl.when(z == planes - 1)
-            def _():
-                from_right[c_left, 1] = part[c_left]
-
-            @pl.when(z < planes - 1)
-            def _():
-                left_copy(c_left).wait_recv()
-                from_right[c_left, 1] = part[c_left] + from_right[c_left, 0]
-
-            @pl.when(z > 0)
-            def _():
-                left_copy(c_left).start()
-
-        @pl.when(i + lead < chunks)
+                @pl.when(z == planes - 1)
+                def _():
+                    from_right[c_left, 1, rows, :] = part[c_left, rows, :]
+
+                @pl.when(z < planes - 1)
+                def _():
+                    left_copy(c_left, h).wait_recv()
+                    from_right[c_left, 1, rows, :] = part[c_left, rows, :] + from_right[c_left, 0, rows, :]
+
+                @pl.when(z > 0)
+                def _():
+                    left_copy(c_left, h).start()
+
+        @pl.when(i + lead < pairs)
         def _():
             send_raw(i + lead, 0)
 
         c = i - lag
 
-        @pl.when((c >= 0) & (c < chunks))
+        @pl.when((c >= 0) & (c < pairs))
         def _():
             coeff = from_left[c, 1] + (from_right[c, 1] - part[c])
             slab[c] = slab[c] - product(pattern, split(coeff))
             for step in range(1, plane):
                 back_copy(c, step).start()
-            land[:, column(q * chunks + c)] = slab[c, own_rows(q), :]
+            land[:, slot(q * pairs + c)] = slab[c, own_rows(q), :]
+
+        @pl.when(i + 1 < pairs)
+        def _():
+            measure_modes(i + 1)
 
         @pl.when(i == 0)
         def _():
             noise_copy.wait()
 
-        @pl.when(i < 4)
+        @pl.when(i < 2)
         def _():
             def regroup(at, carry):
-                row = i * (side // 4) + at
+                row = i * (side // 2) + at
                 out_ref[spread(row), :] = noise_ref[:, column(row)]
                 return carry
 
-            lax.fori_loop(0, side // 4, regroup, 0, unroll=4)
-
-        @pl.when((i >= 4) & (i < 8))
+            lax.fori_loop(0, side // 2, regroup, 0, unroll=4)
+
+        @pl.when((i >= 2) & (i < 4))
         def _():
             def swap(at, carry):
-                det = (i - 4) * (dets // 4) + at
+                det = (i - 2) * (dets // 2) + at
                 fold[pl.ds(det, side, stride=dets), :] = out_ref[column(det), :].T
                 return carry
 
-            lax.fori_loop(0, dets // 4, swap, 0)
-
-        @pl.when(i == 8)
-        def _():
-            def add_mirror(k, carry):
-                high, low = split(fold[own_rows(side - k), :])
+            lax.fori_loop(0, dets // 2, swap, 0, unroll=2)
+
+        @pl.when(i == 3)
+        def _():
+            def add_mirror(at, carry):
+                ks = [1 + at * 3 + j for j in range(3)]
+                high, low = split(jnp.concatenate([fold[own_rows(side - k), :] for k in ks], axis=0))
                 dot = functools.partial(jnp.dot, preferred_element_type=jnp.float32)
-                fold[own_rows(k), :] += dot(high, flip[...]) + dot(low, flip[...])
+                mirror = dot(high, flip[...]) + dot(low, flip[...])
+                for j, k in enumerate(ks):
+                    fold[own_rows(k), :] += mirror[j * dets:(j + 1) * dets]
                 return carry
 
-            lax.fori_loop(1, side // 2, add_mirror, 0)
-
-        pair = (i - mid_lag - 1) // 2
-
-        @pl.when((i > mid_lag) & ((i - mid_lag) % 2 == 1) & (pair < chunks // 2))
+            lax.fori_loop(0, (side // 2 - 1) // 3, add_mirror, 0)
+
+        pair = i - mid_lag
+
+        @pl.when((pair >= 0) & (pair < pairs))
         def _():
             for step in range(1, plane):
-                back_copy(2 * pair, step).wait_recv()
-                back_copy(2 * pair + 1, step).wait_recv()
-            slots = [owner * (chunks // 2) + pair for owner in range(plane)]
+                back_copy(pair, step).wait_recv()
+            slots = [owner * pairs + pair for owner in range(plane)]
             real = [land[:, column(2 * k)] for k in slots]
             imag = [land[:, column(2 * k + 1)] for k in slots]
             for k, (r, m) in zip(slots, middle(real, imag, slots)):
@@ -298,24 +312,26 @@
 
         return carry
 
-    lax.fori_loop(0, chunks + mid_lag + 1, one_step, 0)
-
-    def finish(chunk, carry):
+    lax.fori_loop(0, pairs + mid_lag, one_step, 0)
+
+    def finish(pair, carry):
         for step in range(1, plane):
-            back_copy(chunk, step).wait_send()
-            raw_copy(chunk, step).wait_send()
+            back_copy(pair, step).wait_send()
+            raw_copy(pair, step).wait_send()
 
         @pl.when(z < planes - 1)
         def _():
-            right_copy(chunk).wait_send()
+            for h in range(2):
+                right_copy(pair, h).wait_send()
 
         @pl.when(z > 0)
         def _():
-            left_copy(chunk).wait_send()
+            for h in range(2):
+                left_copy(pair, h).wait_send()
 
         return carry
 
-    lax.fori_loop(0, chunks, finish, 0)
+    lax.fori_loop(0, pairs, finish, 0)
 
 
 def correct(stream, gains, noise, mode_pattern, mode_weights, tables, size):
@@ -324,13 +340,13 @@
     side = math.isqrt(samples)
     plane = 4 if size % 4 == 0 else 1
     planes = size // plane
-    chunks = side // plane
+    pairs = side // plane // 2
     rows = plane * dets
     f32 = jnp.float32
     vmem = pl.BlockSpec(memory_space=pltpu.VMEM)
     sem = pltpu.SemaphoreType.DMA
-    coeffs = pltpu.VMEM((chunks, rank, side), f32)
-    chain = pltpu.VMEM((chunks, 2, rank, side), f32)
+    coeffs = pltpu.VMEM((pairs, rank, 2 * side), f32)
+    chain = pltpu.VMEM((pairs, 2, rank, 2 * side), f32)
     whole = pltpu.VMEM((dets, samples), f32)
     cube = pltpu.VMEM((dets * side, side), f32)
     return pl.pallas_call(
@@ -339,9 +355,9 @@
         in_specs=[vmem, vmem, pl.BlockSpec(memory_space=pl.ANY)] + [vmem] * (2 + len(tables)),
         out_specs=pl.BlockSpec(memory_space=pltpu.VMEM),
         scratch_shapes=[
-            whole, sem(()), cube, whole, pltpu.VMEM((chunks, rows, side), f32), coeffs, chain, chain, whole, cube,
-            sem((chunks, plane)), sem((chunks, plane)), sem((chunks,)), sem((chunks,)),
-            sem((chunks,)), sem((chunks,)), sem((chunks, plane)), sem((chunks, plane)),
+            whole, sem(()), cube, whole, pltpu.VMEM((pairs, rows, 2 * side), f32), coeffs, chain, chain, whole, cube,
+            sem((pairs, plane)), sem((pairs, plane)), sem((pairs, 2)), sem((pairs, 2)),
+            sem((pairs, 2)), sem((pairs, 2)), sem((pairs, plane)), sem((pairs, plane)),
         ],
         compiler_params=pltpu.CompilerParams(
             collective_id=0, has_side_effects=True, vmem_limit_bytes=60 * MIB
@@ -431,81 +447,103 @@
     )(packed, ids, hits, sky_rows, table)
 
 
-def map_kernel(size, acc_ref, count_ref, out_ref, landed, tallies, send_sem, recv_sem, tally_send, tally_recv):
+def map_kernel(
+    plane, planes, acc_ref, count_ref, out_ref,
+    near, near_tally, partial, tally, far, far_tally,
+    near_send, near_recv, near_tally_send, near_tally_recv, far_send, far_recv, far_tally_send, far_tally_recv,
+):
     me = lax.axis_index("det")
-    rows = out_ref.shape[0]
+    z, q = me // plane, me % plane
+    rows, columns = out_ref.shape
     barrier = pltpu.get_barrier_semaphore()
 
-    def greet(step, carry):
-        pl.semaphore_signal(barrier, inc=1, device_id={"det": lax.rem(me + step, size)})
-        return carry
-
-    lax.fori_loop(1, size, greet, 0)
-    pl.semaphore_wait(barrier, size - 1)
-
-    def copy(step):
-        other = lax.rem(me + step, size)
+    def neighbour(step):
+        return z * plane + lax.rem(q + step, plane)
+
+    def beyond(step):
+        return lax.rem(me + step * plane, plane * planes)
+
+    for step in range(1, plane):
+        pl.semaphore_signal(barrier, inc=1, device_id={"det": neighbour(step)})
+    for step in range(1, planes):
+        pl.semaphore_signal(barrier, inc=1, device_id={"det": beyond(step)})
+    pl.semaphore_wait(barrier, plane + planes - 2)
+
+    def share(owner):
+        return pl.ds(pl.multiple_of(owner * rows, 8), rows)
+
+    def remote(source, target, send_sem, recv_sem, device):
         return pltpu.make_async_remote_copy(
-            src_ref=acc_ref.at[pl.ds(pl.multiple_of(other * rows, 8), rows), :],
-            dst_ref=landed.at[step],
-            send_sem=send_sem.at[step],
-            recv_sem=recv_sem.at[step],
-            device_id={"det": other},
+            src_ref=source, dst_ref=target, send_sem=send_sem, recv_sem=recv_sem, device_id={"det": device}
         )
 
-    def tally(step):
-        return pltpu.make_async_remote_copy(
-            src_ref=count_ref,
-            dst_ref=tallies.at[step],
-            send_sem=tally_send.at[step],
-            recv_sem=tally_recv.at[step],
-            device_id={"det": lax.rem(me + step, size)},
-        )
-
-    def start(step, carry):
-        copy(step).start()
-        tally(step).start()
-        return carry
-
-    lax.fori_loop(1, size, start, 0)
-
-    def add(step, total):
-        copy(step).wait_recv()
-        tally(step).wait_recv()
-        return total[0] + landed[step], total[1] + tallies[step]
-
-    own = acc_ref[pl.ds(pl.multiple_of(me * rows, 8), rows), :]
-    sums, counts = lax.fori_loop(1, size, add, (own, count_ref[...]))
+    first, second = [], []
+    for step in range(1, plane):
+        source = acc_ref.at[:, share(lax.rem(q + step, plane)), :]
+        at = step - 1
+        first.append((
+            remote(source, near.at[at], near_send.at[at], near_recv.at[at], neighbour(step)),
+            remote(count_ref, near_tally.at[at], near_tally_send.at[at], near_tally_recv.at[at], neighbour(step)),
+        ))
+    for step in range(1, planes):
+        at = step - 1
+        source = partial.at[lax.rem(z + step, planes)]
+        second.append((
+            remote(source, far.at[at], far_send.at[at], far_recv.at[at], beyond(step)),
+            remote(tally, far_tally.at[at], far_tally_send.at[at], far_tally_recv.at[at], beyond(step)),
+        ))
+    for pair in first:
+        for copy in pair:
+            copy.start()
+    sums, counts = acc_ref[:, share(q), :], count_ref[...]
+    for at, pair in enumerate(first):
+        for copy in pair:
+            copy.wait_recv()
+        sums, counts = sums + near[at], counts + near_tally[at]
+    partial[...] = sums
+    tally[...] = counts
+    for pair in second:
+        for copy in pair:
+            copy.start()
+    sums = partial[z]
+    for at, pair in enumerate(second):
+        for copy in pair:
+            copy.wait_recv()
+        sums, counts = sums + far[at], counts + far_tally[at]
     shape = (rows, counts.shape[1])
     mine = lax.broadcasted_iota(jnp.int32, shape, 1) == lax.broadcasted_iota(jnp.int32, shape, 0) + me * rows
     counts = jnp.sum(jnp.where(mine, counts, 0.0), axis=1, keepdims=True)
     out_ref[...] = sums / jnp.sqrt(1.0 + counts)
-
-    def finish(step, carry):
-        copy(step).wait_send()
-        tally(step).wait_send()
-        return carry
-
-    lax.fori_loop(1, size, finish, 0)
+    for pair in first + second:
+        for copy in pair:
+            copy.wait_send()
 
 
 def combine_map(acc, counts, size):
     blocks, columns = acc.shape
     rows = blocks // size
-    sem = pltpu.SemaphoreType.DMA((size,))
+    plane = 4 if size % 4 == 0 else 1
+    planes = size // plane
+    near, far = max(1, plane - 1), max(1, planes - 1)
+    sems = [pltpu.SemaphoreType.DMA((near,))] * 4 + [pltpu.SemaphoreType.DMA((far,))] * 4
+    f32 = jnp.float32
     return pl.pallas_call(
-        functools.partial(map_kernel, size),
-        out_shape=jax.ShapeDtypeStruct((rows, columns), jnp.float32),
+        functools.partial(map_kernel, plane, planes),
+        out_shape=jax.ShapeDtypeStruct((rows, columns), f32),
         in_specs=[pl.BlockSpec(memory_space=pltpu.VMEM)] * 2,
         out_specs=pl.BlockSpec(memory_space=pltpu.VMEM),
         scratch_shapes=[
-            pltpu.VMEM((size, rows, columns), jnp.float32),
-            pltpu.VMEM((size, 1, blocks), jnp.float32),
-            sem, sem, sem, sem,
+            pltpu.VMEM((near, planes, rows, columns), f32),
+            pltpu.VMEM((near, 1, blocks), f32),
+            pltpu.VMEM((planes, rows, columns), f32),
+            pltpu.VMEM((1, blocks), f32),
+            pltpu.VMEM((far, rows, columns), f32),
+            pltpu.VMEM((far, 1, blocks), f32),
+            *sems,
         ],
         compiler_params=pltpu.CompilerParams(collective_id=1, has_side_effects=True),
         name="combine_map",
-    )(acc, counts)
+    )(acc.reshape(planes, plane * rows, columns), counts)
 
 
 def shards(size, timestream, gains, mode_pattern, mode_weights, noise_weight, block_ids, hits, sky_rows):

time: 164 us -> 161 us (0.982)
  Pallas kernels: 161 us -> 158 us
    pallas_call x1, Pallas kernels: 138 us -> 135 us  [correct(): pl.pallas_call(functools.partial(correct_kernel, plane, planes), out_shap...]
where the time goes in v4:
time: 161 us; the launch traced here: 160 us
  Pallas kernels  158 us (98%)
    pallas_call x1, Pallas kernels, correct(): pl.pallas_call(functools.partial(correct_kernel, plane, planes), out_shap...  135 us
    pallas_call x1, Pallas kernels, combine_map(): pl.pallas_call(functools.partial(map_kernel, plane, planes), out_shape=ja...  12 us
    pallas_call x1, Pallas kernels, finish_and_bin(): pl.pallas_call(bin_kernel, grid=(dets // batch,), out_shape=(jax.ShapeDty...  11.6 us

profile of v4, /device:TPU:0, one launch (start us, length us, event | category | flops | bytes accessed | tf_op | source)
XLA Modules:
  0.0 160.4 jit_solution(9286766961575234150)
XLA Ops:
  0.6 134.8 %correct.1 = f32[8192,128]{1,0:T(8,128)} custom-call(f32[64,16384]{1,0:T(8,128)} %bitcast.8, f32[1,64]{1,0:T(1,128)} %gain_ref.1, f32[64,16384]{1,0:T(8,128)} %noise_hbm.1, f32[1024,256]{1,0:T(8,128)} %weight_ref.1, f32[1024,256]{1,0:T(8,128)} %pattern_ref.1, bf16[2,128,128]{2,1,0:T(8,128)(2,1)} %constant.12.clone.t1, ...), custom_call_target="tpu_custom_call" | custom-call | tf_op jit(solution)/shard_map/correct/pallas_call | solution.py:352
  135.4 11.6 %finish_and_bin.1 = (f32[64,16384]{1,0:T(8,128)}, f32[256,256]{1,0:T(8,128)}, f32[1,256]{1,0:T(1,128)}) custom-call(f32[64,128,128]{2,1,0:T(8,128)} %bitcast.7, s32[64,64]{1,0:T(8,128)} %bitcast.10, s32[64,64]{1,0:T(8,128)} %bitcast.11, s32[1,256]{1,0:T(1,128)} %bitcast.12, bf16[2,128,128]{2,1,0:T(8,128)(2,1)} %constant.17.clone.t4), custom_call_target="tpu_custom_call" | custom-call | tf_op jit(solution)/shard_map/finish_and_bin/pallas_call | solution.py:424
  147.0 12.0 %combine_map.1 = f32[16,256]{1,0:T(8,128)} custom-call(f32[4,64,256]{2,1,0:T(8,128)} %bitcast.9, f32[1,256]{1,0:T(1,128)} %get-tuple-element.7.count_ref), custom_call_target="tpu_custom_call" | custom-call | tf_op jit(solution)/shard_map/combine_map/pallas_call | solution.py:530
  159.0 1.3 copy.17

commit v5 on v4

--- a/solution.py
+++ b/solution.py
@@ -117,12 +117,13 @@
             device_id={"det": z * plane + other},
         )
 
-    halves_of = [pl.ds(h * (rank // 2), rank // 2) for h in range(2)]
+    pieces = 4
+    piece = [pl.ds(h * (rank // pieces), rank // pieces) for h in range(pieces)]
 
     def right_copy(pair, h):
         return pltpu.make_async_remote_copy(
-            src_ref=from_left.at[pair, 1, halves_of[h], :],
-            dst_ref=from_left.at[pair, 0, halves_of[h], :],
+            src_ref=from_left.at[pair, 1, piece[h], :],
+            dst_ref=from_left.at[pair, 0, piece[h], :],
             send_sem=right_send.at[pair, h],
             recv_sem=right_recv.at[pair, h],
             device_id={"det": lax.rem(me + plane, plane * planes)},
@@ -130,8 +131,8 @@
 
     def left_copy(pair, h):
         return pltpu.make_async_remote_copy(
-            src_ref=from_right.at[pair, 1, halves_of[h], :],
-            dst_ref=from_right.at[pair, 0, halves_of[h], :],
+            src_ref=from_right.at[pair, 1, piece[h], :],
+            dst_ref=from_right.at[pair, 0, piece[h], :],
             send_sem=left_send.at[pair, h],
             recv_sem=left_recv.at[pair, h],
             device_id={"det": lax.rem(me + plane * (planes - 1), plane * planes)},
@@ -204,8 +205,9 @@
     def one_step(i, carry):
         c_right = i - z
         c_left = i - (planes - 1 - z)
-        for h in range(2):
-            rows = halves_of[h]
+
+        def chain(h):
+            rows = piece[h]
 
             @pl.when((c_right >= 0) & (c_right < pairs))
             def _():
@@ -237,23 +239,17 @@
                 def _():
                     left_copy(c_left, h).start()
 
+        chain(0)
+
+        @pl.when(i + 1 < pairs)
+        def _():
+            measure_modes(i + 1)
+
         @pl.when(i + lead < pairs)
         def _():
             send_raw(i + lead, 0)
 
-        c = i - lag
-
-        @pl.when((c >= 0) & (c < pairs))
-        def _():
-            coeff = from_left[c, 1] + (from_right[c, 1] - part[c])
-            slab[c] = slab[c] - product(pattern, split(coeff))
-            for step in range(1, plane):
-                back_copy(c, step).start()
-            land[:, slot(q * pairs + c)] = slab[c, own_rows(q), :]
-
-        @pl.when(i + 1 < pairs)
-        def _():
-            measure_modes(i + 1)
+        chain(1)
 
         @pl.when(i == 0)
         def _():
@@ -290,6 +286,8 @@
 
             lax.fori_loop(0, (side // 2 - 1) // 3, add_mirror, 0)
 
+        chain(2)
+
         pair = i - mid_lag
 
         @pl.when((pair >= 0) & (pair < pairs))
@@ -310,6 +308,17 @@
                 out_ref[spread(0), :] = ends[0][0]
                 out_ref[spread(1), :] = ends[1][0]
 
+        chain(3)
+        c = i - lag
+
+        @pl.when((c >= 0) & (c < pairs))
+        def _():
+            coeff = from_left[c, 1] + (from_right[c, 1] - part[c])
+            slab[c] = slab[c] - product(pattern, split(coeff))
+            for step in range(1, plane):
+                back_copy(c, step).start()
+            land[:, slot(q * pairs + c)] = slab[c, own_rows(q), :]
+
         return carry
 
     lax.fori_loop(0, pairs + mid_lag, one_step, 0)
@@ -321,12 +330,12 @@
 
         @pl.when(z < planes - 1)
         def _():
-            for h in range(2):
+            for h in range(pieces):
                 right_copy(pair, h).wait_send()
 
         @pl.when(z > 0)
         def _():
-            for h in range(2):
+            for h in range(pieces):
                 left_copy(pair, h).wait_send()
 
         return carry
@@ -356,8 +365,8 @@
         out_specs=pl.BlockSpec(memory_space=pltpu.VMEM),
         scratch_shapes=[
             whole, sem(()), cube, whole, pltpu.VMEM((pairs, rows, 2 * side), f32), coeffs, chain, chain, whole, cube,
-            sem((pairs, plane)), sem((pairs, plane)), sem((pairs, 2)), sem((pairs, 2)),
-            sem((pairs, 2)), sem((pairs, 2)), sem((pairs, plane)), sem((pairs, plane)),
+            sem((pairs, plane)), sem((pairs, plane)), sem((pairs, 4)), sem((pairs, 4)),
+            sem((pairs, 4)), sem((pairs, 4)), sem((pairs, plane)), sem((pairs, plane)),
         ],
         compiler_params=pltpu.CompilerParams(
             collective_id=0, has_side_effects=True, vmem_limit_bytes=60 * MIB
@@ -366,7 +375,7 @@
     )(stream, gains, noise, mode_weights, mode_pattern, *tables)
 
 
-def bin_kernel(x_ref, id_ref, hit_ref, sky_ref, t4, out_ref, acc_ref, count_ref, rows_ref):
+def bin_kernel(x_ref, id_ref, hit_ref, sky_ref, t4, out_ref, acc_ref, count_ref, rows_ref, hits_ref):
     batch, side, _ = x_ref.shape
     per_row = PIX // side
     tiles = side // per_row
@@ -386,18 +395,20 @@
     ladder = lax.broadcasted_iota(jnp.int32, (blocks, batch * tiles), 0)
     ids = jnp.concatenate([id_ref[b:b + 1, :] for b in range(batch)], axis=1)
     hits = jnp.concatenate([hit_ref[b:b + 1, :] for b in range(batch)], axis=1).astype(jnp.float32)
-    table = jnp.where(ids == ladder, hits, 0.0).astype(jnp.bfloat16)
+    table = jnp.where(ids == ladder, hits, 0.0)
+    counts = table[:, :LANES]
+    for at in range(LANES, batch * tiles, LANES):
+        counts = counts + table[:, at:at + LANES]
+    table = table.astype(jnp.bfloat16)
     dot = functools.partial(jnp.dot, preferred_element_type=jnp.float32)
-    ones = jnp.ones((8, batch * tiles), jnp.bfloat16)
-    counts = lax.dot_general(ones, table, (((1,), (1,)), ((), ())), preferred_element_type=jnp.float32)
 
     @pl.when(pl.program_id(0) == 0)
     def _():
         acc_ref[...] = jnp.zeros_like(acc_ref)
-        count_ref[...] = jnp.zeros_like(count_ref)
+        hits_ref[...] = jnp.zeros_like(hits_ref)
 
     acc_ref[...] += dot(table, high) + dot(table, low)
-    count_ref[...] += counts[:1]
+    hits_ref[...] += counts
 
     @pl.when(pl.program_id(0) == pl.num_programs(0) - 1)
     def _():
@@ -407,17 +418,18 @@
         high, low = split(total)
         rest = (total - high.astype(jnp.float32) - low.astype(jnp.float32)).astype(jnp.bfloat16)
         acc_ref[...] = dot(place, high) + (dot(place, low) + dot(place, rest))
-        tally = jnp.broadcast_to(count_ref[...], (8, blocks))
+        high, low = split(hits_ref[...])
+        tally = split(dot(place, high) + dot(place, low))
+        ones = jnp.ones((8, LANES), jnp.bfloat16)
         across = functools.partial(
             lax.dot_general, dimension_numbers=(((1,), (1,)), ((), ())), preferred_element_type=jnp.float32
         )
-        high, low = split(tally)
-        count_ref[...] = (across(high, place) + across(low, place))[:1]
+        count_ref[...] = (across(ones, tally[0]) + across(ones, tally[1]))[:1]
 
 
 def finish_and_bin(packed, ids, hits, sky_rows, table):
     dets, side, _ = packed.shape
-    batch = 8
+    batch = 16 if dets % 16 == 0 else 8
     tiles = side * side // PIX
     blocks = sky_rows.shape[1]
     line = pl.BlockSpec((batch, tiles), lambda i: (i, 0))
@@ -441,7 +453,7 @@
             pl.BlockSpec((blocks, PIX), lambda i: (0, 0)),
             pl.BlockSpec((1, blocks), lambda i: (0, 0)),
         ),
-        scratch_shapes=[pltpu.VMEM((batch * side, side), jnp.float32)],
+        scratch_shapes=[pltpu.VMEM((batch * side, side), jnp.float32), pltpu.VMEM((blocks, LANES), jnp.float32)],
         compiler_params=pltpu.CompilerParams(vmem_limit_bytes=60 * MIB),
         name="finish_and_bin",
     )(packed, ids, hits, sky_rows, table)

time: 161 us -> 164 us (1.019)
  Pallas kernels: 158 us -> 162 us
    pallas_call x1, Pallas kernels: 135 us -> 138 us  [correct(): pl.pallas_call(functools.partial(correct_kernel, plane, planes), out_shap...]
where the time goes in v5:
time: 164 us; the launch traced here: 163 us
  Pallas kernels  162 us (99%)
    pallas_call x1, Pallas kernels, correct(): pl.pallas_call(functools.partial(correct_kernel, plane, planes), out_shap...  138 us
    pallas_call x1, Pallas kernels, combine_map(): pl.pallas_call(functools.partial(map_kernel, plane, planes), out_shape=ja...  13.4 us
    pallas_call x1, Pallas kernels, finish_and_bin(): pl.pallas_call(bin_kernel, grid=(dets // batch,), out_shape=(jax.ShapeDty...  10.2 us

profile of v5, /device:TPU:0, one launch (start us, length us, event | category | flops | bytes accessed | tf_op | source)
XLA Modules:
  0.0 163.5 jit_solution(2353699852744296475)
XLA Ops:
  0.6 138.0 %correct.1 = f32[8192,128]{1,0:T(8,128)} custom-call(f32[64,16384]{1,0:T(8,128)} %bitcast.8, f32[1,64]{1,0:T(1,128)} %gain_ref.1, f32[64,16384]{1,0:T(8,128)} %noise_hbm.1, f32[1024,256]{1,0:T(8,128)} %weight_ref.1, f32[1024,256]{1,0:T(8,128)} %pattern_ref.1, bf16[2,128,128]{2,1,0:T(8,128)(2,1)} %constant.12.clone.t1, ...), custom_call_target="tpu_custom_call" | custom-call | tf_op jit(solution)/shard_map/correct/pallas_call | solution.py:361
  138.6 10.2 %finish_and_bin.1 = (f32[64,16384]{1,0:T(8,128)}, f32[256,256]{1,0:T(8,128)}, f32[1,256]{1,0:T(1,128)}) custom-call(f32[64,128,128]{2,1,0:T(8,128)} %bitcast.7, s32[64,64]{1,0:T(8,128)} %bitcast.10, s32[64,64]{1,0:T(8,128)} %bitcast.11, s32[1,256]{1,0:T(1,128)} %bitcast.12, bf16[2,128,128]{2,1,0:T(8,128)(2,1)} %constant.17.clone.t4), custom_call_target="tpu_custom_call" | custom-call | tf_op jit(solution)/shard_map/finish_and_bin/pallas_call | solution.py:436
  148.8 13.4 %combine_map.1 = f32[16,256]{1,0:T(8,128)} custom-call(f32[4,64,256]{2,1,0:T(8,128)} %bitcast.9, f32[1,256]{1,0:T(1,128)} %get-tuple-element.7.count_ref), custom_call_target="tpu_custom_call" | custom-call | tf_op jit(solution)/shard_map/combine_map/pallas_call | solution.py:542
  162.2 1.3 copy.17

commit v6 on v4

--- a/solution.py
+++ b/solution.py
@@ -21,8 +21,11 @@
 
 
 def product(left, right):
-    dot = functools.partial(jnp.dot, preferred_element_type=jnp.float32)
-    return dot(left[0], right[0]) + (dot(left[0], right[1]) + dot(left[1], right[0]))
+    high, low = left
+    left = jnp.concatenate([high, high, low], axis=1)
+    high, low = right
+    right = jnp.concatenate([high, low, high], axis=0)
+    return jnp.dot(left, right, preferred_element_type=jnp.float32)
 
 
 def halves(table):
@@ -366,7 +369,7 @@
     )(stream, gains, noise, mode_weights, mode_pattern, *tables)
 
 
-def bin_kernel(x_ref, id_ref, hit_ref, sky_ref, t4, out_ref, acc_ref, count_ref, rows_ref):
+def bin_kernel(x_ref, id_ref, hit_ref, sky_ref, t4, out_ref, acc_ref, count_ref, rows_ref, hits_ref):
     batch, side, _ = x_ref.shape
     per_row = PIX // side
     tiles = side // per_row
@@ -386,18 +389,20 @@
     ladder = lax.broadcasted_iota(jnp.int32, (blocks, batch * tiles), 0)
     ids = jnp.concatenate([id_ref[b:b + 1, :] for b in range(batch)], axis=1)
     hits = jnp.concatenate([hit_ref[b:b + 1, :] for b in range(batch)], axis=1).astype(jnp.float32)
-    table = jnp.where(ids == ladder, hits, 0.0).astype(jnp.bfloat16)
+    table = jnp.where(ids == ladder, hits, 0.0)
+    counts = table[:, :LANES]
+    for at in range(LANES, batch * tiles, LANES):
+        counts = counts + table[:, at:at + LANES]
+    table = table.astype(jnp.bfloat16)
     dot = functools.partial(jnp.dot, preferred_element_type=jnp.float32)
-    ones = jnp.ones((8, batch * tiles), jnp.bfloat16)
-    counts = lax.dot_general(ones, table, (((1,), (1,)), ((), ())), preferred_element_type=jnp.float32)
 
     @pl.when(pl.program_id(0) == 0)
     def _():
         acc_ref[...] = jnp.zeros_like(acc_ref)
-        count_ref[...] = jnp.zeros_like(count_ref)
+        hits_ref[...] = jnp.zeros_like(hits_ref)
 
     acc_ref[...] += dot(table, high) + dot(table, low)
-    count_ref[...] += counts[:1]
+    hits_ref[...] += counts
 
     @pl.when(pl.program_id(0) == pl.num_programs(0) - 1)
     def _():
@@ -407,17 +412,18 @@
         high, low = split(total)
         rest = (total - high.astype(jnp.float32) - low.astype(jnp.float32)).astype(jnp.bfloat16)
         acc_ref[...] = dot(place, high) + (dot(place, low) + dot(place, rest))
-        tally = jnp.broadcast_to(count_ref[...], (8, blocks))
+        high, low = split(hits_ref[...])
+        tally = split(dot(place, high) + dot(place, low))
+        ones = jnp.ones((8, LANES), jnp.bfloat16)
         across = functools.partial(
             lax.dot_general, dimension_numbers=(((1,), (1,)), ((), ())), preferred_element_type=jnp.float32
         )
-        high, low = split(tally)
-        count_ref[...] = (across(high, place) + across(low, place))[:1]
+        count_ref[...] = (across(ones, tally[0]) + across(ones, tally[1]))[:1]
 
 
 def finish_and_bin(packed, ids, hits, sky_rows, table):
     dets, side, _ = packed.shape
-    batch = 8
+    batch = 16 if dets % 16 == 0 else 8
     tiles = side * side // PIX
     blocks = sky_rows.shape[1]
     line = pl.BlockSpec((batch, tiles), lambda i: (i, 0))
@@ -441,7 +447,7 @@
             pl.BlockSpec((blocks, PIX), lambda i: (0, 0)),
             pl.BlockSpec((1, blocks), lambda i: (0, 0)),
         ),
-        scratch_shapes=[pltpu.VMEM((batch * side, side), jnp.float32)],
+        scratch_shapes=[pltpu.VMEM((batch * side, side), jnp.float32), pltpu.VMEM((blocks, LANES), jnp.float32)],
         compiler_params=pltpu.CompilerParams(vmem_limit_bytes=60 * MIB),
         name="finish_and_bin",
     )(packed, ids, hits, sky_rows, table)

time: 161 us -> 158 us (0.981)
  Pallas kernels: 158 us -> 156 us
    pallas_call x1, Pallas kernels: 11.6 us -> 9.59 us  [finish_and_bin(): pl.pallas_call(bin_kernel, grid=(dets // batch,), out_shape=(jax.ShapeDty...]
where the time goes in v6:
time: 158 us
  Pallas kernels  156 us (99%)
    pallas_call x1, Pallas kernels, correct(): pl.pallas_call(functools.partial(correct_kernel, plane, planes), out_shap...  134 us
    pallas_call x1, Pallas kernels, combine_map(): pl.pallas_call(functools.partial(map_kernel, plane, planes), out_shape=ja...  12.1 us
    pallas_call x1, Pallas kernels, finish_and_bin(): pl.pallas_call(bin_kernel, grid=(dets // batch,), out_shape=(jax.ShapeDty...  9.59 us

profile of v6, /device:TPU:0, one launch (start us, length us, event | category | flops | bytes accessed | tf_op | source)
XLA Modules:
  0.0 158.0 jit_solution(4720975433131814749)
XLA Ops:
  0.6 134.4 %correct.1 = f32[8192,128]{1,0:T(8,128)} custom-call(f32[64,16384]{1,0:T(8,128)} %bitcast.8, f32[1,64]{1,0:T(1,128)} %gain_ref.1, f32[64,16384]{1,0:T(8,128)} %noise_hbm.1, f32[1024,256]{1,0:T(8,128)} %weight_ref.1, f32[1024,256]{1,0:T(8,128)} %pattern_ref.1, bf16[2,128,128]{2,1,0:T(8,128)(2,1)} %constant.12.clone.t1, ...), custom_call_target="tpu_custom_call" | custom-call | tf_op jit(solution)/shard_map/correct/pallas_call | solution.py:355
  135.0 9.6 %finish_and_bin.1 = (f32[64,16384]{1,0:T(8,128)}, f32[256,256]{1,0:T(8,128)}, f32[1,256]{1,0:T(1,128)}) custom-call(f32[64,128,128]{2,1,0:T(8,128)} %bitcast.7, s32[64,64]{1,0:T(8,128)} %bitcast.10, s32[64,64]{1,0:T(8,128)} %bitcast.11, s32[1,256]{1,0:T(1,128)} %bitcast.12, bf16[2,128,128]{2,1,0:T(8,128)(2,1)} %constant.17.clone.t4), custom_call_target="tpu_custom_call" | custom-call | tf_op jit(solution)/shard_map/finish_and_bin/pallas_call | solution.py:430
  144.6 12.1 %combine_map.1 = f32[16,256]{1,0:T(8,128)} custom-call(f32[4,64,256]{2,1,0:T(8,128)} %bitcast.9, f32[1,256]{1,0:T(1,128)} %get-tuple-element.7.count_ref), custom_call_target="tpu_custom_call" | custom-call | tf_op jit(solution)/shard_map/combine_map/pallas_call | solution.py:536
  156.7 1.3 copy.17

commit v7 on v6

--- a/solution.py
+++ b/solution.py
@@ -67,7 +67,9 @@
     pairs = side // plane // 2
     rank = part.shape[1]
     lag = planes - 1
-    mid_lag = max(lag + 1, 4)
+    ready = 8
+    mid_lag = lag + 1
+    assert mid_lag >= ready or (mid_lag == ready // 2 and pairs >= ready)
     lead = min(3, pairs)
     noise_copy = pltpu.make_async_copy(noise_hbm, noise_ref, noise_sem)
     noise_copy.start()
@@ -271,32 +273,35 @@
 
             lax.fori_loop(0, side // 2, regroup, 0, unroll=4)
 
-        @pl.when((i >= 2) & (i < 4))
+        @pl.when((i >= 2) & (i < 6))
         def _():
             def swap(at, carry):
-                det = (i - 2) * (dets // 2) + at
+                det = (i - 2) * (dets // 4) + at
                 fold[pl.ds(det, side, stride=dets), :] = out_ref[column(det), :].T
                 return carry
 
-            lax.fori_loop(0, dets // 2, swap, 0, unroll=2)
-
-        @pl.when(i == 3)
-        def _():
-            def add_mirror(at, carry):
-                ks = [1 + at * 3 + j for j in range(3)]
-                high, low = split(jnp.concatenate([fold[own_rows(side - k), :] for k in ks], axis=0))
-                dot = functools.partial(jnp.dot, preferred_element_type=jnp.float32)
-                mirror = dot(high, flip[...]) + dot(low, flip[...])
-                for j, k in enumerate(ks):
-                    fold[own_rows(k), :] += mirror[j * dets:(j + 1) * dets]
-                return carry
-
-            lax.fori_loop(0, (side // 2 - 1) // 3, add_mirror, 0)
-
-        pair = i - mid_lag
-
-        @pl.when((pair >= 0) & (pair < pairs))
-        def _():
+            lax.fori_loop(0, dets // 4, swap, 0, unroll=2)
+
+        def add_mirror(at, carry):
+            ks = [1 + at * 3 + j for j in range(3)]
+            high, low = split(jnp.concatenate([fold[own_rows(side - k), :] for k in ks], axis=0))
+            dot = functools.partial(jnp.dot, preferred_element_type=jnp.float32)
+            mirror = dot(high, flip[...]) + dot(low, flip[...])
+            for j, k in enumerate(ks):
+                fold[own_rows(k), :] += mirror[j * dets:(j + 1) * dets]
+            return carry
+
+        triples = (side // 2 - 1) // 3
+
+        @pl.when(i == 6)
+        def _():
+            lax.fori_loop(0, triples // 2, add_mirror, 0)
+
+        @pl.when(i == 7)
+        def _():
+            lax.fori_loop(triples // 2, triples, add_mirror, 0)
+
+        def transform(pair, carry):
             for step in range(1, plane):
                 back_copy(pair, step).wait_recv()
             slots = [owner * pairs + pair for owner in range(plane)]
@@ -312,6 +317,16 @@
                 ends = middle([real[0], imag[0]], [none, none], [0, side // 2])
                 out_ref[spread(0), :] = ends[0][0]
                 out_ref[spread(1), :] = ends[1][0]
+            return carry
+
+        @pl.when((i >= max(mid_lag, ready + (ready - mid_lag) * (mid_lag < ready))) & (i < pairs + mid_lag))
+        def _():
+            transform(i - mid_lag, 0)
+
+        if mid_lag < ready:
+            @pl.when((i >= ready) & (i < ready + ready // 2))
+            def _():
+                lax.fori_loop(2 * (i - ready), 2 * (i - ready) + 2, transform, 0)
 
         return carry
 

time: 158 us -> 154 us (0.975)
  Pallas kernels: 156 us -> 152 us
    pallas_call x1, Pallas kernels: 134 us -> 130 us  [correct(): pl.pallas_call(functools.partial(correct_kernel, plane, planes), out_shap...]
where the time goes in v7:
time: 154 us; the launch traced here: 153 us
  Pallas kernels  152 us (99%)
    pallas_call x1, Pallas kernels, correct(): pl.pallas_call(functools.partial(correct_kernel, plane, planes), out_shap...  130 us
    pallas_call x1, Pallas kernels, combine_map(): pl.pallas_call(functools.partial(map_kernel, plane, planes), out_shape=ja...  11.6 us
    pallas_call x1, Pallas kernels, finish_and_bin(): pl.pallas_call(bin_kernel, grid=(dets // batch,), out_shape=(jax.ShapeDty...  9.6 us

profile of v7, /device:TPU:0, one launch (start us, length us, event | category | flops | bytes accessed | tf_op | source)
XLA Modules:
  0.0 153.5 jit_solution(14001019403293419546)
XLA Ops:
  0.6 130.3 %correct.1 = f32[8192,128]{1,0:T(8,128)} custom-call(f32[64,16384]{1,0:T(8,128)} %bitcast.8, f32[1,64]{1,0:T(1,128)} %gain_ref.1, f32[64,16384]{1,0:T(8,128)} %noise_hbm.1, f32[1024,256]{1,0:T(8,128)} %weight_ref.1, f32[1024,256]{1,0:T(8,128)} %pattern_ref.1, bf16[2,128,128]{2,1,0:T(8,128)(2,1)} %constant.12.clone.t1, ...), custom_call_target="tpu_custom_call" | custom-call | tf_op jit(solution)/shard_map/correct/pallas_call | solution.py:370
  131.0 9.6 %finish_and_bin.1 = (f32[64,16384]{1,0:T(8,128)}, f32[256,256]{1,0:T(8,128)}, f32[1,256]{1,0:T(1,128)}) custom-call(f32[64,128,128]{2,1,0:T(8,128)} %bitcast.7, s32[64,64]{1,0:T(8,128)} %bitcast.10, s32[64,64]{1,0:T(8,128)} %bitcast.11, s32[1,256]{1,0:T(1,128)} %bitcast.12, bf16[2,128,128]{2,1,0:T(8,128)(2,1)} %constant.17.clone.t4), custom_call_target="tpu_custom_call" | custom-call | tf_op jit(solution)/shard_map/finish_and_bin/pallas_call | solution.py:445
  140.6 11.6 %combine_map.1 = f32[16,256]{1,0:T(8,128)} custom-call(f32[4,64,256]{2,1,0:T(8,128)} %bitcast.9, f32[1,256]{1,0:T(1,128)} %get-tuple-element.7.count_ref), custom_call_target="tpu_custom_call" | custom-call | tf_op jit(solution)/shard_map/combine_map/pallas_call | solution.py:551
  152.2 1.3 copy.17
